TPU v7x, 256 devices: a whole 4x4x8 slice. The times are simulated.
256 devices in a mesh: tm: 64 (over z, y, core), chan: 4 (over x).
Axes of the slice: x: 4, y: 4, z: 8, core: 2. Of those that a mesh axis runs over, the one named last changes fastest.
Arguments:
- tokens: bfloat16 [65536, 1024], P('tm', 'chan'), may hold values from -180 to 180
- norm_gain: float32 [1024], replicated, may hold values from 0.25 to 1.75
- w_value: bfloat16 [1024, 1024], P(None, 'chan'), may hold values from -0.1875 to 0.1875
- w_gate: bfloat16 [1024, 1024], P(None, 'chan'), may hold values from -0.1875 to 0.1875
- phi_taps: float32 [32, 512], replicated, may hold values from -0.0625 to 0.0625
- tap_coeff: float32 [32, 1024], P(None, 'chan'), may hold values from -6 to 6
- skip_gain: float32 [1024], P('chan'), may hold values from -6 to 6
- basis_up: float32 [16, 256], replicated, may hold values from -0.375 to 0.375
- basis_down: float32 [16, 256], replicated, may hold values from -1.5 to 1.5
- lift_maps: float32 [6, 2, 16, 16], replicated, may hold values from -1 to 1
- spread_maps: float32 [6, 2, 16, 16], replicated, may hold values from -1.5 to 1.5
- couplings: float32 [7, 2, 16, 16, 1024], P(None, None, None, None, 'chan'), may hold values from -1 to 1
Outputs:
- filtered: bfloat16 [65536, 1024], P('tm', 'chan')
All inputs are finite; a program needn't handle non-finite values.
Results may differ from a plain program's by a relative error of at most 0.007.
Values may be sent and summed in bfloat16 or wider, within the bound.
A program may use at most 128 MiB of HBM per device.

v0:
```python
import jax
import jax.numpy as jnp
import numpy as np
from jax import lax
from jax.experimental import pallas as pl
from jax.experimental.pallas import tpu as pltpu
from jax.sharding import PartitionSpec as P

MESH = pl.DeviceIdType.MESH
F32 = jnp.float32
BF16 = jnp.bfloat16
HIGHEST = lax.Precision.HIGHEST

LEAF = 256
LEAVES = 4
WIDTH = 256
RANK = 16
PLANES = 8
PLANE = 8


def transform_tables():
    odd = np.arange(LEAF)[:, None] + 0.5
    angle = 2 * np.pi * odd * np.arange(LEAF)[None, :] / (2 * LEAF)
    forward = np.concatenate([np.cos(angle), -np.sin(angle)], 0)
    return forward.astype(np.float32), (forward.T / LEAF).astype(np.float32)


def exact_dot(left, right):
    return jnp.dot(left, right, precision=HIGHEST, preferred_element_type=F32)


def dot(left, right):
    return jnp.dot(left, right, preferred_element_type=F32)


def halves(value):
    high = value.astype(BF16)
    return high, (value - high.astype(F32)).astype(BF16)


def selector(lanes, period, shift, limit):
    row = lax.broadcasted_iota(jnp.int32, (RANK, lanes), 0)
    lane = lax.broadcasted_iota(jnp.int32, (RANK, lanes), 1)
    return ((lax.rem(lane, period) == row + shift) & (lane < limit)).astype(F32)


def body(
    tok, gain, w_value, w_gate, phi, coeff, skip, up, down, lift, spread, coup, fwd, inv,
    out,
    g, w, gain_v, phi_v, coeff_v, skip_v, up_v, down_v, lift_v, spread_v, coup_v, fwd_f, inv_f, fwd_v, inv_v,
    vals, halo, gate, near, spec, khat, mom_m, lift_m, six_m, far_m, red_m, moms,
    m2, m2_prev, ctx_out, ctx_in, pack_out, pack_in, m5_in, far0, far1, out_v, parts, part_squares,
    local_sem, dsend, drecv, rsend, rrecv, hsem, csem, s1, r1, s1p, r1p, s2, r2, s5, r5, ready_plane, ready_next, ready_edge, ready_later, osem,
):
    t = lax.axis_index("tm")
    x = lax.axis_index("chan")
    core = lax.rem(t, 2)
    y = lax.rem(lax.div(t, 2), 4)
    z = lax.div(t, PLANE)
    own = lax.rem(t, PLANE)
    right, left = lax.rem(x + 1, 4), lax.rem(x + 3, 4)

    barrier = pltpu.get_barrier_semaphore()

    def signal(semaphore, frames, chans):
        pl.semaphore_signal(semaphore, inc=1, device_id=(frames, chans), device_id_type=MESH)

    signal(barrier, t, right)
    signal(barrier, t, left)

    @pl.when(z < PLANES - 1)
    def _():
        signal(barrier, t + PLANE, x)

    for k in range(1, PLANE):

        @pl.when(own + k < PLANE)
        def _():
            signal(barrier, t + k, x)

    m2_prev[...] = jnp.zeros_like(m2_prev)
    ctx_in[...] = jnp.zeros_like(ctx_in)
    pack_in[...] = jnp.zeros_like(pack_in)
    m5_in[...] = jnp.zeros_like(m5_in)
    halo[...] = jnp.zeros_like(halo)

    pl.semaphore_wait(barrier, 2 + own + jnp.where(z > 0, 1, 0))

    owners = [x, left, right, lax.rem(x + 2, 4)]

    def leaf_rows(leaf):
        return pl.ds(leaf * LEAF if isinstance(leaf, int) else pl.multiple_of(leaf * LEAF, LEAF), LEAF)

    def direct(group, way):
        rows = pl.ds((1 - group) * 2 * LEAF, 2 * LEAF)
        return pltpu.make_async_remote_copy(
            src_ref=tok.at[rows],
            dst_ref=g.at[1 + way, rows],
            send_sem=dsend.at[way, group],
            recv_sem=drecv.at[way, group],
            device_id=(t, left if way else right),
            device_id_type=MESH,
        )

    def relay(group, way):
        rows = leaf_rows((1 - group) * 2 + way)
        return pltpu.make_async_remote_copy(
            src_ref=g.at[1 + way, rows],
            dst_ref=g.at[3, rows],
            send_sem=rsend.at[way, group],
            recv_sem=rrecv.at[way, group],
            device_id=(t, left if way else right),
            device_id_type=MESH,
        )

    def send_direct(group):
        for way in range(2):
            direct(group, way).start()

    def pass_on(group):
        for way in range(2):
            direct(group, way).wait_recv()
            relay(group, way).start()

    def wait_relayed(group):
        for way in range(2):
            relay(group, way).wait_recv()

    def tables_near():
        for name in ("phi", "coeff", "fwd"):
            copies[name].wait()
        fwd_v[...] = jnp.concatenate(halves(fwd_f[...]), 1)
        taps = phi_v[...].astype(BF16).astype(F32)
        kernel_taps = lax.dot_general(
            taps, coeff_v[...], (((0,), (0,)), ((), ())), precision=HIGHEST, preferred_element_type=F32
        )
        both = jnp.concatenate([kernel_taps[:LEAF], kernel_taps[LEAF:]], 1)
        high, low = halves(both)
        hat = dot(fwd_v[...], jnp.concatenate([high, high], 0)) + dot(fwd_v[:, :LEAF], low)
        a_re, a_im = hat[:LEAF, :WIDTH], hat[LEAF:, :WIDTH]
        b_re, b_im = hat[:LEAF, WIDTH:], hat[LEAF:, WIDTH:]
        row = lax.broadcasted_iota(jnp.int32, (LEAF, WIDTH), 0)
        sign = (1 - 2 * lax.rem(row, 2)).astype(F32)
        khat[0] = a_re
        khat[1] = a_im
        khat[2] = b_re - sign * a_im
        khat[3] = b_im + sign * a_re

    def tables_moments():
        copies["up"].wait()
        copies["lift"].wait()
        base = up_v[...]
        first = [exact_dot(lift_v[0, k], base) for k in range(2)]
        for leaf in range(LEAVES):
            second = exact_dot(lift_v[1, leaf // 2], first[leaf % 2])
            high, low = halves(jnp.concatenate([base, first[leaf % 2], second], 0))
            mom_m[leaf] = jnp.concatenate([high, low], 1)

    def tables_lift():
        def pair(level):
            return exact_dot(lift_v[level, 0], selector(128, 32, 0, 128)) + exact_dot(
                lift_v[level, 1], selector(128, 32, 16, 128)
            )

        def blocks(level, copies_of):
            rows = jnp.concatenate([pair(level)] * copies_of, 0)
            row = lax.broadcasted_iota(jnp.int32, rows.shape, 0)
            lane = lax.broadcasted_iota(jnp.int32, rows.shape, 1)
            return jnp.where(lax.div(row, RANK) == lax.div(lane, 2 * RANK), rows, 0.0)

        three = blocks(2, 8)
        four = exact_dot(blocks(3, 2), three)
        five = exact_dot(blocks(4, 1), jnp.concatenate([four, jnp.zeros((96, 128), F32)], 0))
        whole = jnp.concatenate([four, three[32:64], five, three[:32]], 0)
        high, low = halves(whole)
        lift_m[...] = jnp.concatenate([high, low], 1)
        six = exact_dot(lift_v[5, 0], selector(128, 32, 0, 64)) + exact_dot(
            lift_v[5, 1], selector(128, 32, 16, 64)
        )
        high = six.astype(BF16).astype(F32)
        lane = lax.broadcasted_iota(jnp.int32, six.shape, 1)
        six_m[...] = jnp.where(lane < 32, high, six - high).astype(BF16)

    def tables_far():
        copies["spread"].wait()
        copies["down"].wait()
        row = lax.broadcasted_iota(jnp.int32, (RANK, LEAF), 0)
        lane = lax.broadcasted_iota(jnp.int32, (RANK, LEAF), 1)
        summing = (lax.div(lane, RANK) == row).astype(F32)
        chain = None
        for k in range(5):
            if k > 0:
                step = spread_v[1 + k, lax.rem(lax.div(t, 2 ** (k - 1)), 2)]
                chain = step if k == 1 else exact_dot(chain, step)
            high, low = halves(summing if k == 0 else exact_dot(chain, summing))
            red_m[k] = jnp.concatenate([high, low], 0)
        for leaf in range(LEAVES):
            near_step = spread_v[0, leaf % 2]
            both_steps = exact_dot(near_step, spread_v[1, leaf // 2])
            mix = (
                selector(LEAF, 48, 0, 144)
                + exact_dot(near_step, selector(LEAF, 48, 16, 144))
                + exact_dot(both_steps, selector(LEAF, 48, 32, 144))
            )
            whole = lax.dot_general(
                down_v[...], mix, (((0,), (0,)), ((), ())), precision=HIGHEST, preferred_element_type=F32
            )
            high = whole.astype(BF16).astype(F32)
            lane_at = lax.broadcasted_iota(jnp.int32, whole.shape, 1)
            far_m[leaf] = jnp.where(lane_at < 96, high, whole - high).astype(BF16)

    def scaled_rows(leaf, slots):
        rows = leaf_rows(leaf)
        squares = jnp.zeros((LEAF, WIDTH), F32)
        columns = []
        for slot in slots:
            tokens = g[slot, rows, :].astype(F32)
            squares = squares + tokens * tokens
            scale = gain_v[:, pl.ds(pl.multiple_of(owners[slot] * WIDTH, WIDTH), WIDTH)]
            columns.append((tokens * scale).astype(BF16))
        return jnp.concatenate(columns, 1), squares

    def gather_part(leaf):
        scaled, squares = scaled_rows(leaf, (0, 1, 2))
        parts[leaf] = dot(scaled, w[:3].reshape(3 * WIDTH, 2 * WIDTH))
        part_squares[leaf] = squares[:, : WIDTH // 2] + squares[:, WIDTH // 2 :]

    def values_of(leaf):
        scaled, squares = scaled_rows(leaf, (3,))
        squares = squares[:, : WIDTH // 2] + squares[:, WIDTH // 2 :] + part_squares[leaf]
        inverse = lax.rsqrt(jnp.sum(squares, axis=1, keepdims=True) / 1024 + 1e-06)
        part_squares[leaf] = jnp.broadcast_to(inverse, squares.shape)
        value = ((parts[leaf, :, :WIDTH] + dot(scaled, w[3, :, :WIDTH])) * inverse).astype(BF16)
        vals[leaf_rows(leaf), :] = value
        moms[leaf] = dot(mom_m[leaf], jnp.concatenate([value, value], 0))

    def gates_of(leaf):
        scaled, _ = scaled_rows(leaf, (3,))
        inverse = part_squares[leaf]
        sums = parts[leaf, :, WIDTH:] + dot(scaled, w[3, :, WIDTH:])
        gate[leaf_rows(leaf), :] = jax.nn.sigmoid(sums * jnp.concatenate([inverse, inverse], 1))

    def spectrum_of(leaf):
        value = vals[leaf_rows(leaf), :]
        spec[leaf] = dot(fwd_v[...], jnp.concatenate([value, value], 0))

    def near_rows(leaf):
        rows = leaf_rows(leaf)
        before = (leaf - 1 if leaf > 0 else LEAVES) if isinstance(leaf, int) else leaf - 1
        a_re, a_im = spec[leaf, :LEAF, :], spec[leaf, LEAF:, :]
        b_re, b_im = spec[before, :LEAF, :], spec[before, LEAF:, :]
        out_re = khat[0] * a_re - khat[1] * a_im + khat[2] * b_re - khat[3] * b_im
        out_im = khat[0] * a_im + khat[1] * a_re + khat[2] * b_im + khat[3] * b_re
        both = jnp.concatenate([out_re, out_im], 0).astype(BF16)
        total = dot(inv_v[...], jnp.concatenate([both, both], 0))
        near[rows, :] = total + skip_v[...] * vals[rows, :].astype(F32)

    def coupled(level, source_two, source_three):
        product = coup_v[level, 0] * source_two[None]
        if source_three is not None:
            product = product + coup_v[level, 1] * source_three[None]
        return product.reshape(RANK * RANK, WIDTH).astype(BF16)

    send_direct(0)

    copies = {}

    def local(name, source, target):
        copies[name] = pltpu.make_async_copy(source, target, local_sem.at[len(copies)])
        copies[name].start()

    local("tok", tok, g.at[0])
    for slot in range(4):
        rows = pl.ds(pl.multiple_of(owners[slot] * WIDTH, WIDTH), WIDTH)
        local(("v", slot), w_value.at[rows], w.at[slot, :, pl.ds(0, WIDTH)])
        local(("g", slot), w_gate.at[rows], w.at[slot, :, pl.ds(WIDTH, WIDTH)])
    for name, source, target in (
        ("gain", gain, gain_v),
        ("phi", phi, phi_v),
        ("coeff", coeff, coeff_v),
        ("fwd", fwd, fwd_f),
        ("skip", skip, skip_v),
        ("up", up, up_v),
        ("down", down, down_v),
        ("lift", lift, lift_v),
        ("spread", spread, spread_v),
        ("inv", inv, inv_f),
        ("coup", coup, coup_v),
    ):
        local(name, source, target)

    @pl.when(z > 0)
    def _():
        signal(ready_next, t - PLANE, x)

    for k in range(1, PLANE):

        @pl.when(own >= k)
        def _():
            signal(ready_plane, t - k, x)

    def chain(place):
        @pl.when(z == PLANES - 1 - place)
        def _():
            if not isinstance(place, int) or place > 0:
                pl.semaphore_wait(ready_later, 1)
            if not isinstance(place, int) or place < PLANES - 1:
                signal(ready_later, t - PLANE, x)

    def over(first, last, work):
        def step(leaf, carry):
            work(leaf)
            return carry

        lax.fori_loop(first, last, step, 0)

    chain(0)
    tables_near()
    send_direct(1)
    chain(1)
    tables_moments()
    tables_lift()
    chain(2)

    @pl.when(own < PLANE - 1)
    def _():
        pl.semaphore_wait(ready_plane, PLANE - 1 - own)

    @pl.when(z < PLANES - 1)
    def _():
        pl.semaphore_wait(ready_next, 1)

        @pl.when(y == 0)
        def _():
            signal(ready_edge, z * PLANE + 6, x)
            signal(ready_edge, z * PLANE + 7, x)

    for slot in range(4):
        copies["v", slot].wait()
        copies["g", slot].wait()
    for name in ("tok", "gain", "skip", "coup", "inv"):
        copies[name].wait()
    chain(3)
    pass_on(0)
    chain(4)
    over(2, 4, gather_part)
    tables_far()
    inv_v[...] = jnp.concatenate(halves(inv_f[...]), 1)
    chain(5)

    @pl.when((y == 3) & (z < PLANES - 1))
    def _():
        pl.semaphore_wait(ready_edge, 2)

    pass_on(1)
    chain(6)
    over(0, 2, gather_part)
    chain(7)

    halo_copy = pltpu.make_async_remote_copy(
        src_ref=vals.at[pl.ds(3 * LEAF, LEAF)],
        dst_ref=halo,
        send_sem=hsem.at[0],
        recv_sem=hsem.at[1],
        device_id=(t + 1, x),
        device_id_type=MESH,
    )

    ctx_copy = pltpu.make_async_remote_copy(
        src_ref=ctx_out,
        dst_ref=ctx_in,
        send_sem=csem.at[0],
        recv_sem=csem.at[1],
        device_id=(t + 1, x),
        device_id_type=MESH,
    )

    wait_relayed(0)
    over(2, 4, values_of)

    @pl.when(t < PLANES * PLANE - 1)
    def _():
        halo_copy.start()

    over(2, 4, spectrum_of)
    over(2, 4, gates_of)
    near_rows(3)

    wait_relayed(1)
    over(0, 2, values_of)

    total = moms[0, 32:48, :] + moms[1, 32:48, :] + moms[2, 32:48, :] + moms[3, 32:48, :]
    m2[own] = total.astype(BF16)

    def plane_copy(k):
        return pltpu.make_async_remote_copy(
            src_ref=m2.at[own],
            dst_ref=m2.at[own],
            send_sem=s1.at[k - 1],
            recv_sem=r1.at[k - 1],
            device_id=(z * PLANE + lax.rem(own + k, PLANE), x),
            device_id_type=MESH,
        )

    def plane_arrival(k):
        return pltpu.make_async_remote_copy(
            src_ref=m2.at[own],
            dst_ref=m2.at[lax.rem(own + PLANE - k, PLANE)],
            send_sem=s1.at[k - 1],
            recv_sem=r1.at[k - 1],
            device_id=(z * PLANE + lax.rem(own + k, PLANE), x),
            device_id_type=MESH,
        )

    for k in range(1, PLANE):
        plane_copy(k).start()

    def next_plane_copy(target, source):
        return pltpu.make_async_remote_copy(
            src_ref=m2.at[own],
            dst_ref=m2_prev.at[source],
            send_sem=s1p.at[target],
            recv_sem=r1p.at[source],
            device_id=((z + 1) * PLANE + target, x),
            device_id_type=MESH,
        )

    @pl.when((y == 3) & (z < PLANES - 1))
    def _():
        for target in range(2):
            next_plane_copy(target, core).start()

    ctx_out[...] = jnp.concatenate(
        [
            moms[2, 0:16, :],
            moms[3, 0:16, :],
            moms[0, 16:32, :] + moms[1, 16:32, :],
            moms[2, 16:32, :] + moms[3, 16:32, :],
        ],
        0,
    ).astype(BF16)

    @pl.when(t < PLANES * PLANE - 1)
    def _():
        ctx_copy.start()

    over(0, 2, gates_of)

    for k in range(1, PLANE):
        plane_arrival(k).wait_recv()
    stack = m2[...].reshape(PLANE * RANK, WIDTH)
    lifted = dot(lift_m[...], jnp.concatenate([stack, stack], 0))
    pack_out[...] = lifted[:80].astype(BF16)


    def pack_copy(rows):
        return pltpu.make_async_remote_copy(
            src_ref=pack_out.at[pl.ds(0, rows)],
            dst_ref=pack_in.at[pl.ds(0, rows)],
            send_sem=s2,
            recv_sem=r2,
            device_id=(t + PLANE, x),
            device_id_type=MESH,
        )

    def five_copy(k):
        return pltpu.make_async_remote_copy(
            src_ref=pack_out.at[pl.ds(64, RANK)],
            dst_ref=m5_in.at[k],
            send_sem=s5.at[k],
            recv_sem=r5.at[k],
            device_id=(t + k * PLANE, x),
            device_id_type=MESH,
        )

    @pl.when((z < PLANES - 1) & (y < 2))
    def _():
        pack_copy(64).start()

    @pl.when((z < PLANES - 1) & (y >= 2))
    def _():
        pack_copy(32).start()

    for k in range(2, PLANES):

        @pl.when(z + k < PLANES)
        def _():
            five_copy(k).start()

    over(0, 2, spectrum_of)
    over(1, 3, near_rows)

    @pl.when(t > 0)
    def _():
        halo_copy.wait_recv()

    before = halo[...]
    spec[LEAVES] = dot(fwd_v[...], jnp.concatenate([before, before], 0))
    near_rows(0)

    summing = red_m[0, :RANK, :]

    def gathered(level, source_two, source_three=None):
        return dot(summing, coupled(level, source_two, source_three))

    @pl.when(t > 0)
    def _():
        ctx_copy.wait_recv()

    prev = ctx_in[...].astype(F32)
    far0[0] = gathered(0, prev[0:16])
    far0[1] = gathered(0, prev[16:32], prev[0:16])
    far0[2] = gathered(0, moms[0, 0:16, :])
    far0[3] = gathered(0, moms[1, 0:16, :], moms[0, 0:16, :])
    far1[0] = gathered(1, prev[32:48])
    far1[1] = gathered(1, prev[48:64], prev[32:48])

    for way in range(2):
        for group in range(2):
            direct(group, way).wait_send()
            relay(group, way).wait_send()

    for k in range(1, PLANE):
        plane_copy(k).wait_send()

    @pl.when(t < PLANES * PLANE - 1)
    def _():
        halo_copy.wait_send()
        ctx_copy.wait_send()

    @pl.when((y == 3) & (z < PLANES - 1))
    def _():
        for target in range(2):
            next_plane_copy(target, core).wait_send()

    @pl.when((y == 0) & (z > 0))
    def _():
        for source in range(2):
            next_plane_copy(source, source).wait_recv()

    def reduced(k, source_two, source_three):
        return dot(red_m[k], coupled(2 + k, source_two, source_three))

    at = 2 * jnp.maximum(y - 1, 0)
    inside = y > 0
    two = jnp.where(inside, m2[at + core], m2_prev[core]).astype(F32)
    three = jnp.where(inside, m2[at], m2_prev[0]).astype(F32) * core.astype(F32)
    expansion = reduced(0, two, three)

    @pl.when((z > 0) & (y < 2))
    def _():
        pack_copy(64).wait_recv()

    @pl.when((z > 0) & (y >= 2))
    def _():
        pack_copy(32).wait_recv()

    odd = lax.rem(y, 2)
    lower = y < 2
    here = jnp.where(odd == 1, lifted[96:112], lifted[80:96])
    coming = pack_in[pl.ds(pl.multiple_of(32 + odd * RANK, RANK), RANK), :].astype(F32)
    two = jnp.where(lower, coming, here)
    three = jnp.where(lower, pack_in[32:48, :].astype(F32), lifted[80:96]) * odd.astype(F32)
    expansion = expansion + reduced(1, two, three)
    odd = lax.div(y, 2)
    two = pack_in[pl.ds(pl.multiple_of(odd * RANK, RANK), RANK), :].astype(F32)
    three = pack_in[0:16, :].astype(F32) * odd.astype(F32)
    expansion = expansion + reduced(2, two, three)

    for k in range(2, PLANES):

        @pl.when(z >= k)
        def _():
            five_copy(k).wait_recv()

    odd = lax.rem(z, 2)
    expansion = expansion + reduced(
        3, m5_in[2].astype(F32), m5_in[3].astype(F32) * odd.astype(F32)
    )
    pad = jnp.zeros((64, WIDTH), BF16)

    def sixth(base):
        pair = [m5_in[base], m5_in[base - 1]]
        return dot(six_m[...], jnp.concatenate(pair + pair + [pad], 0))

    odd_six = lax.rem(lax.div(z, 2), 2)
    expansion = expansion + reduced(
        4, sixth(4 + odd), sixth(6 + odd) * odd_six.astype(F32)
    )

    expansion = expansion[:RANK] + expansion[RANK:]

    def out_copy(leaf):
        rows = leaf_rows(leaf)
        return pltpu.make_async_copy(out_v.at[rows], out.at[rows], osem.at[leaf])

    for leaf in range(LEAVES):
        rows = leaf_rows(leaf)
        high, low = halves(jnp.concatenate([far0[leaf], far1[leaf // 2], expansion], 0))
        whole = jnp.concatenate([high, low, high, jnp.zeros((112, WIDTH), BF16)], 0)
        combined = near[rows, :] + dot(far_m[leaf], whole)
        out_v[rows, :] = (gate[rows, :] * combined).astype(BF16)
        out_copy(leaf).start()

    @pl.when((z < PLANES - 1) & (y < 2))
    def _():
        pack_copy(64).wait_send()

    @pl.when((z < PLANES - 1) & (y >= 2))
    def _():
        pack_copy(32).wait_send()

    for k in range(2, PLANES):

        @pl.when(z + k < PLANES)
        def _():
            five_copy(k).wait_send()

    for leaf in range(LEAVES):
        out_copy(leaf).wait()


def per_device(
    tokens,
    norm_gain,
    w_value,
    w_gate,
    phi_taps,
    tap_coeff,
    skip_gain,
    basis_up,
    basis_down,
    lift_maps,
    spread_maps,
    couplings,
):
    forward, inverse = transform_tables()
    in_hbm = pl.BlockSpec(memory_space=pltpu.HBM)
    frames = LEAF * LEAVES
    vmem = pltpu.VMEM
    dma = pltpu.SemaphoreType.DMA
    scratch = [
        vmem((4, frames, WIDTH), BF16),
        vmem((4, WIDTH, 2 * WIDTH), BF16),
        vmem((1, 4 * WIDTH), F32),
        vmem(phi_taps.shape, F32),
        vmem(tap_coeff.shape, F32),
        vmem((1, WIDTH), F32),
        vmem(basis_up.shape, F32),
        vmem(basis_down.shape, F32),
        vmem(lift_maps.shape, F32),
        vmem(spread_maps.shape, F32),
        vmem(couplings.shape, F32),
        vmem(forward.shape, F32),
        vmem(inverse.shape, F32),
        vmem((2 * LEAF, 2 * LEAF), BF16),
        vmem((LEAF, 4 * LEAF), BF16),
        vmem((frames, WIDTH), BF16),
        vmem((LEAF, WIDTH), BF16),
        vmem((frames, WIDTH), F32),
        vmem((frames, WIDTH), F32),
        vmem((LEAVES + 1, 2 * LEAF, WIDTH), F32),
        vmem((4, LEAF, WIDTH), F32),
        vmem((LEAVES, 48, 2 * LEAF), BF16),
        vmem((112, 256), BF16),
        vmem((RANK, 128), BF16),
        vmem((LEAVES, LEAF, LEAF), BF16),
        vmem((5, 2 * RANK, LEAF), BF16),
        vmem((LEAVES, 48, WIDTH), F32),
        vmem((PLANE, RANK, WIDTH), BF16),
        vmem((2, RANK, WIDTH), BF16),
        vmem((64, WIDTH), BF16),
        vmem((64, WIDTH), BF16),
        vmem((80, WIDTH), BF16),
        vmem((64, WIDTH), BF16),
        vmem((PLANES, RANK, WIDTH), BF16),
        vmem((LEAVES, RANK, WIDTH), F32),
        vmem((2, RANK, WIDTH), F32),
        vmem((frames, WIDTH), BF16),
        vmem((LEAVES, LEAF, 2 * WIDTH), F32),
        vmem((LEAVES, LEAF, WIDTH // 2), F32),
        dma((20,)),
        dma((2, 2)),
        dma((2, 2)),
        dma((2, 2)),
        dma((2, 2)),
        dma((2,)),
        dma((2,)),
        dma((PLANE - 1,)),
        dma((PLANE - 1,)),
        dma((2,)),
        dma((2,)),
        dma(()),
        dma(()),
        dma((PLANES,)),
        dma((PLANES,)),
        pltpu.SemaphoreType.REGULAR,
        pltpu.SemaphoreType.REGULAR,
        pltpu.SemaphoreType.REGULAR,
        pltpu.SemaphoreType.REGULAR,
        dma((LEAVES,)),
    ]
    return pl.pallas_call(
        body,
        out_shape=jax.ShapeDtypeStruct(tokens.shape, BF16),
        in_specs=[in_hbm] * 14,
        out_specs=in_hbm,
        scratch_shapes=scratch,
        compiler_params=pltpu.CompilerParams(
            collective_id=0, has_side_effects=True, vmem_limit_bytes=60 * 1024 * 1024
        ),
        cost_estimate=pl.CostEstimate(flops=4 * 10**9, bytes_accessed=8 * 10**6, transcendentals=10**6),
    )(
        tokens,
        norm_gain.reshape(1, -1),
        w_value,
        w_gate,
        phi_taps,
        tap_coeff,
        skip_gain.reshape(1, -1),
        basis_up,
        basis_down,
        lift_maps,
        spread_maps,
        couplings,
        jnp.asarray(forward),
        jnp.asarray(inverse),
    )


def solution(mesh):
    placed = (
        P("tm", "chan"),
        P(),
        P(None, "chan"),
        P(None, "chan"),
        P(),
        P(None, "chan"),
        P("chan"),
        P(),
        P(),
        P(),
        P(),
        P(None, None, None, None, "chan"),
    )
    return jax.shard_map(
        per_device, mesh=mesh, in_specs=placed, out_specs=P("tm", "chan"), check_vma=False
    )
```

profile of v0, /device:TPU:224, one launch (start us, length us, event | category | flops | bytes accessed | tf_op | source)
XLA Modules:
  0.0 36.3 jit_solution(1030351161073222971)
XLA Ops:
  0.0 34.4 %shard_map.136 = bf16[1024,256]{1,0:T(8,128)(2,1)} custom-call(bf16[1024,256]{1,0:T(8,128)(2,1)} %tok.1, f32[1,1024]{1,0:T(1,128)} %bitcast.2, bf16[1024,256]{1,0:T(8,128)(2,1)} %w_value.1, bf16[1024,256]{1,0:T(8,128)(2,1)} %w_gate.1, f32[32,512]{1,0:T(8,128)} %phi.1, f32[32,256]{1,0:T(8,128)} %coeff.1, f32[1,256]{1,0:T(1,128)} %bitcast.3, f32[16,256]{1,0:T(8,128)} %up.1, ...), custom_call_target="tpu_custom_call" | custom-call | flops 4000000000 | bytes 8000000 | tf_op jit(solution)/shard_map/pallas_call | solution.py:704
  34.4 1.9 %copy.16 = bf16[1024,256]{1,0:T(8,128)(2,1)} copy(bf16[1024,256]{1,0:T(8,128)(2,1)} %shard_map.136) | data formatting | bytes 1048576
where the time goes:
time: 36.4 us; the launch traced here: 36.3 us
  Pallas kernels  34.4 us (95%)
  local copies, waits for them, and re-layouts  1.87 us (5%)
    pallas_call x1, Pallas kernels, per_device(): pl.pallas_call(body, out_shape=jax.ShapeDtypeStruct(tokens.shape, BF16),...  34.4 us
    unnamed x1, local copies, waits for them, and re-layouts  1.87 us

commit v1 on v0

--- a/solution.py
+++ b/solution.py
@@ -9,7 +9,6 @@
 MESH = pl.DeviceIdType.MESH
 F32 = jnp.float32
 BF16 = jnp.bfloat16
-HIGHEST = lax.Precision.HIGHEST
 
 LEAF = 256
 LEAVES = 4
@@ -26,10 +25,6 @@
     return forward.astype(np.float32), (forward.T / LEAF).astype(np.float32)
 
 
-def exact_dot(left, right):
-    return jnp.dot(left, right, precision=HIGHEST, preferred_element_type=F32)
-
-
 def dot(left, right):
     return jnp.dot(left, right, preferred_element_type=F32)
 
@@ -37,6 +32,18 @@
 def halves(value):
     high = value.astype(BF16)
     return high, (value - high.astype(F32)).astype(BF16)
+
+
+def fine_dot(left, right):
+    left_high, left_low = halves(left)
+    right_high, right_low = halves(right)
+    return dot(left_high, right_high) + dot(left_high, right_low) + dot(left_low, right_high)
+
+
+def place_dot(left, right):
+    left_high, left_low = halves(left)
+    ones = right.astype(BF16)
+    return dot(left_high, ones) + dot(left_low, ones)
 
 
 def selector(lanes, period, shift, limit):
@@ -131,10 +138,9 @@
         for name in ("phi", "coeff", "fwd"):
             copies[name].wait()
         fwd_v[...] = jnp.concatenate(halves(fwd_f[...]), 1)
-        taps = phi_v[...].astype(BF16).astype(F32)
-        kernel_taps = lax.dot_general(
-            taps, coeff_v[...], (((0,), (0,)), ((), ())), precision=HIGHEST, preferred_element_type=F32
-        )
+        taps = phi_v[...].astype(BF16).astype(F32).T.astype(BF16)
+        coeff_high, coeff_low = halves(coeff_v[...])
+        kernel_taps = dot(taps, coeff_high) + dot(taps, coeff_low)
         both = jnp.concatenate([kernel_taps[:LEAF], kernel_taps[LEAF:]], 1)
         high, low = halves(both)
         hat = dot(fwd_v[...], jnp.concatenate([high, high], 0)) + dot(fwd_v[:, :LEAF], low)
@@ -151,15 +157,15 @@
         copies["up"].wait()
         copies["lift"].wait()
         base = up_v[...]
-        first = [exact_dot(lift_v[0, k], base) for k in range(2)]
+        first = [fine_dot(lift_v[0, k], base) for k in range(2)]
         for leaf in range(LEAVES):
-            second = exact_dot(lift_v[1, leaf // 2], first[leaf % 2])
+            second = fine_dot(lift_v[1, leaf // 2], first[leaf % 2])
             high, low = halves(jnp.concatenate([base, first[leaf % 2], second], 0))
             mom_m[leaf] = jnp.concatenate([high, low], 1)
 
     def tables_lift():
         def pair(level):
-            return exact_dot(lift_v[level, 0], selector(128, 32, 0, 128)) + exact_dot(
+            return place_dot(lift_v[level, 0], selector(128, 32, 0, 128)) + place_dot(
                 lift_v[level, 1], selector(128, 32, 16, 128)
             )
 
@@ -170,12 +176,12 @@
             return jnp.where(lax.div(row, RANK) == lax.div(lane, 2 * RANK), rows, 0.0)
 
         three = blocks(2, 8)
-        four = exact_dot(blocks(3, 2), three)
-        five = exact_dot(blocks(4, 1), jnp.concatenate([four, jnp.zeros((96, 128), F32)], 0))
+        four = fine_dot(blocks(3, 2), three)
+        five = fine_dot(blocks(4, 1), jnp.concatenate([four, jnp.zeros((96, 128), F32)], 0))
         whole = jnp.concatenate([four, three[32:64], five, three[:32]], 0)
         high, low = halves(whole)
         lift_m[...] = jnp.concatenate([high, low], 1)
-        six = exact_dot(lift_v[5, 0], selector(128, 32, 0, 64)) + exact_dot(
+        six = place_dot(lift_v[5, 0], selector(128, 32, 0, 64)) + place_dot(
             lift_v[5, 1], selector(128, 32, 16, 64)
         )
         high = six.astype(BF16).astype(F32)
@@ -192,20 +198,19 @@
         for k in range(5):
             if k > 0:
                 step = spread_v[1 + k, lax.rem(lax.div(t, 2 ** (k - 1)), 2)]
-                chain = step if k == 1 else exact_dot(chain, step)
-            high, low = halves(summing if k == 0 else exact_dot(chain, summing))
+                chain = step if k == 1 else fine_dot(chain, step)
+            high, low = halves(summing if k == 0 else place_dot(chain, summing))
             red_m[k] = jnp.concatenate([high, low], 0)
+        turned = down_v[...].T
         for leaf in range(LEAVES):
             near_step = spread_v[0, leaf % 2]
-            both_steps = exact_dot(near_step, spread_v[1, leaf // 2])
+            both_steps = fine_dot(near_step, spread_v[1, leaf // 2])
             mix = (
                 selector(LEAF, 48, 0, 144)
-                + exact_dot(near_step, selector(LEAF, 48, 16, 144))
-                + exact_dot(both_steps, selector(LEAF, 48, 32, 144))
+                + place_dot(near_step, selector(LEAF, 48, 16, 144))
+                + place_dot(both_steps, selector(LEAF, 48, 32, 144))
             )
-            whole = lax.dot_general(
-                down_v[...], mix, (((0,), (0,)), ((), ())), precision=HIGHEST, preferred_element_type=F32
-            )
+            whole = fine_dot(turned, mix)
             high = whole.astype(BF16).astype(F32)
             lane_at = lax.broadcasted_iota(jnp.int32, whole.shape, 1)
             far_m[leaf] = jnp.where(lane_at < 96, high, whole - high).astype(BF16)
@@ -474,19 +479,19 @@
             device_id_type=MESH,
         )
 
-    @pl.when((z < PLANES - 1) & (y < 2))
-    def _():
-        pack_copy(64).start()
-
-    @pl.when((z < PLANES - 1) & (y >= 2))
-    def _():
-        pack_copy(32).start()
-
-    for k in range(2, PLANES):
+    for k in range(PLANES - 1, 1, -1):
 
         @pl.when(z + k < PLANES)
         def _():
             five_copy(k).start()
+
+    @pl.when((z < PLANES - 1) & (y < 2))
+    def _():
+        pack_copy(64).start()
+
+    @pl.when((z < PLANES - 1) & (y >= 2))
+    def _():
+        pack_copy(32).start()
 
     over(0, 2, spectrum_of)
     over(1, 3, near_rows)

time: 36.4 us -> 35.6 us (0.978)
  Pallas kernels: 34.4 us -> 33.4 us
    pallas_call x1, Pallas kernels: 34.4 us -> 33.4 us  [per_device(): pl.pallas_call(body, out_shape=jax.ShapeDtypeStruct(tokens.shape, BF16),...]
where the time goes in v1:
time: 35.6 us; the launch traced here: 35.2 us
  Pallas kernels  33.4 us (94%)
  local copies, waits for them, and re-layouts  1.87 us (5%)
    pallas_call x1, Pallas kernels, per_device(): pl.pallas_call(body, out_shape=jax.ShapeDtypeStruct(tokens.shape, BF16),...  33.4 us
    unnamed x1, local copies, waits for them, and re-layouts  1.87 us

profile of v1, /device:TPU:224, one launch (start us, length us, event | category | flops | bytes accessed | tf_op | source)
XLA Modules:
  0.0 35.2 jit_solution(36241323004096121)
XLA Ops:
  0.0 33.4 %shard_map.136 = bf16[1024,256]{1,0:T(8,128)(2,1)} custom-call(bf16[1024,256]{1,0:T(8,128)(2,1)} %tok.1, f32[1,1024]{1,0:T(1,128)} %bitcast.2, bf16[1024,256]{1,0:T(8,128)(2,1)} %w_value.1, bf16[1024,256]{1,0:T(8,128)(2,1)} %w_gate.1, f32[32,512]{1,0:T(8,128)} %phi.1, f32[32,256]{1,0:T(8,128)} %coeff.1, f32[1,256]{1,0:T(1,128)} %bitcast.3, f32[16,256]{1,0:T(8,128)} %up.1, ...), custom_call_target="tpu_custom_call" | custom-call | flops 4000000000 | bytes 8000000 | tf_op jit(solution)/shard_map/pallas_call | solution.py:709
  33.4 1.9 %copy.16 = bf16[1024,256]{1,0:T(8,128)(2,1)} copy(bf16[1024,256]{1,0:T(8,128)(2,1)} %shard_map.136) | data formatting | bytes 1048576

commit v2 on v1

--- a/solution.py
+++ b/solution.py
@@ -58,7 +58,7 @@
     g, w, gain_v, phi_v, coeff_v, skip_v, up_v, down_v, lift_v, spread_v, coup_v, fwd_f, inv_f, fwd_v, inv_v,
     vals, halo, gate, near, spec, khat, mom_m, lift_m, six_m, far_m, red_m, moms,
     m2, m2_prev, ctx_out, ctx_in, pack_out, pack_in, m5_in, far0, far1, out_v, parts, part_squares,
-    local_sem, dsend, drecv, rsend, rrecv, hsem, csem, s1, r1, s1p, r1p, s2, r2, s5, r5, ready_plane, ready_next, ready_edge, ready_later, osem,
+    local_sem, gsend, drecv, rrecv, hsem, csem, s1, r1, s1p, r1p, s2, r2, s5, r5, ready_plane, ready_next, ready_edge, ready_later, osem,
 ):
     t = lax.axis_index("tm")
     x = lax.axis_index("chan")
@@ -99,13 +99,13 @@
     def leaf_rows(leaf):
         return pl.ds(leaf * LEAF if isinstance(leaf, int) else pl.multiple_of(leaf * LEAF, LEAF), LEAF)
 
-    def direct(group, way):
-        rows = pl.ds((1 - group) * 2 * LEAF, 2 * LEAF)
+    def direct(piece, way):
+        rows = pl.ds(2 * LEAF, 2 * LEAF) if piece == 0 else leaf_rows(way if piece == 1 else 1 - way)
         return pltpu.make_async_remote_copy(
             src_ref=tok.at[rows],
             dst_ref=g.at[1 + way, rows],
-            send_sem=dsend.at[way, group],
-            recv_sem=drecv.at[way, group],
+            send_sem=gsend,
+            recv_sem=drecv.at[way, piece],
             device_id=(t, left if way else right),
             device_id_type=MESH,
         )
@@ -115,15 +115,15 @@
         return pltpu.make_async_remote_copy(
             src_ref=g.at[1 + way, rows],
             dst_ref=g.at[3, rows],
-            send_sem=rsend.at[way, group],
+            send_sem=gsend,
             recv_sem=rrecv.at[way, group],
             device_id=(t, left if way else right),
             device_id_type=MESH,
         )
 
-    def send_direct(group):
+    def send_direct(piece):
         for way in range(2):
-            direct(group, way).start()
+            direct(piece, way).start()
 
     def pass_on(group):
         for way in range(2):
@@ -348,8 +348,10 @@
         copies[name].wait()
     chain(3)
     pass_on(0)
+    send_direct(2)
     chain(4)
     over(2, 4, gather_part)
+    pass_on(1)
     tables_far()
     inv_v[...] = jnp.concatenate(halves(inv_f[...]), 1)
     chain(5)
@@ -358,7 +360,8 @@
     def _():
         pl.semaphore_wait(ready_edge, 2)
 
-    pass_on(1)
+    for way in range(2):
+        direct(2, way).wait_recv()
     chain(6)
     over(0, 2, gather_part)
     chain(7)
@@ -402,21 +405,20 @@
         return pltpu.make_async_remote_copy(
             src_ref=m2.at[own],
             dst_ref=m2.at[own],
-            send_sem=s1.at[k - 1],
-            recv_sem=r1.at[k - 1],
+            send_sem=s1,
+            recv_sem=r1,
             device_id=(z * PLANE + lax.rem(own + k, PLANE), x),
             device_id_type=MESH,
         )
 
-    def plane_arrival(k):
-        return pltpu.make_async_remote_copy(
-            src_ref=m2.at[own],
-            dst_ref=m2.at[lax.rem(own + PLANE - k, PLANE)],
-            send_sem=s1.at[k - 1],
-            recv_sem=r1.at[k - 1],
-            device_id=(z * PLANE + lax.rem(own + k, PLANE), x),
-            device_id_type=MESH,
-        )
+    plane_all = pltpu.make_async_remote_copy(
+        src_ref=m2.at[pl.ds(0, PLANE - 1)],
+        dst_ref=m2.at[pl.ds(0, PLANE - 1)],
+        send_sem=s1,
+        recv_sem=r1,
+        device_id=(t, right),
+        device_id_type=MESH,
+    )
 
     for k in range(1, PLANE):
         plane_copy(k).start()
@@ -452,8 +454,11 @@
 
     over(0, 2, gates_of)
 
-    for k in range(1, PLANE):
-        plane_arrival(k).wait_recv()
+    early = jnp.where(y == 0, 2, jnp.where(y == 1, 1, 0))
+    over(0, jnp.minimum(2 * early, 2), spectrum_of)
+    over(1, 1 + early, near_rows)
+
+    plane_all.wait_recv()
     stack = m2[...].reshape(PLANE * RANK, WIDTH)
     lifted = dot(lift_m[...], jnp.concatenate([stack, stack], 0))
     pack_out[...] = lifted[:80].astype(BF16)
@@ -493,8 +498,8 @@
     def _():
         pack_copy(32).start()
 
-    over(0, 2, spectrum_of)
-    over(1, 3, near_rows)
+    over(jnp.minimum(2 * early, 2), 2, spectrum_of)
+    over(1 + early, 3, near_rows)
 
     @pl.when(t > 0)
     def _():
@@ -521,13 +526,17 @@
     far1[0] = gathered(1, prev[32:48])
     far1[1] = gathered(1, prev[48:64], prev[32:48])
 
-    for way in range(2):
-        for group in range(2):
-            direct(group, way).wait_send()
-            relay(group, way).wait_send()
-
-    for k in range(1, PLANE):
-        plane_copy(k).wait_send()
+    gather_sent = g.at[pl.ds(0, 3)]
+    pltpu.make_async_remote_copy(
+        src_ref=gather_sent,
+        dst_ref=gather_sent,
+        send_sem=gsend,
+        recv_sem=drecv.at[0, 0],
+        device_id=(t, right),
+        device_id_type=MESH,
+    ).wait_send()
+
+    plane_all.wait_send()
 
     @pl.when(t < PLANES * PLANE - 1)
     def _():
@@ -686,14 +695,13 @@
         vmem((LEAVES, LEAF, 2 * WIDTH), F32),
         vmem((LEAVES, LEAF, WIDTH // 2), F32),
         dma((20,)),
-        dma((2, 2)),
-        dma((2, 2)),
-        dma((2, 2)),
+        dma(()),
+        dma((2, 3)),
         dma((2, 2)),
         dma((2,)),
         dma((2,)),
-        dma((PLANE - 1,)),
-        dma((PLANE - 1,)),
+        dma(()),
+        dma(()),
         dma((2,)),
         dma((2,)),
         dma(()),

time: 35.6 us -> 35.9 us (level)
  Pallas kernels: 33.4 us -> 33.9 us
    pallas_call x1, Pallas kernels: 33.4 us -> 33.9 us  [per_device(): pl.pallas_call(body, out_shape=jax.ShapeDtypeStruct(tokens.shape, BF16),...]
where the time goes in v2:
time: 35.9 us; the launch traced here: 35.8 us
  Pallas kernels  33.9 us (94%)
  local copies, waits for them, and re-layouts  1.87 us (5%)
    pallas_call x1, Pallas kernels, per_device(): pl.pallas_call(body, out_shape=jax.ShapeDtypeStruct(tokens.shape, BF16),...  33.9 us
    unnamed x1, local copies, waits for them, and re-layouts  1.87 us

profile of v2, /device:TPU:224, one launch (start us, length us, event | category | flops | bytes accessed | tf_op | source)
XLA Modules:
  0.0 35.8 jit_solution(13863539343717660159)
XLA Ops:
  0.0 33.9 %shard_map.136 = bf16[1024,256]{1,0:T(8,128)(2,1)} custom-call(bf16[1024,256]{1,0:T(8,128)(2,1)} %tok.1, f32[1,1024]{1,0:T(1,128)} %bitcast.2, bf16[1024,256]{1,0:T(8,128)(2,1)} %w_value.1, bf16[1024,256]{1,0:T(8,128)(2,1)} %w_gate.1, f32[32,512]{1,0:T(8,128)} %phi.1, f32[32,256]{1,0:T(8,128)} %coeff.1, f32[1,256]{1,0:T(1,128)} %bitcast.3, f32[16,256]{1,0:T(8,128)} %up.1, ...), custom_call_target="tpu_custom_call" | custom-call | flops 4000000000 | bytes 8000000 | tf_op jit(solution)/shard_map/pallas_call | solution.py:717
  33.9 1.9 %copy.16 = bf16[1024,256]{1,0:T(8,128)(2,1)} copy(bf16[1024,256]{1,0:T(8,128)(2,1)} %shard_map.136) | data formatting | bytes 1048576

commit v3 on v2

--- a/solution.py
+++ b/solution.py
@@ -99,13 +99,13 @@
     def leaf_rows(leaf):
         return pl.ds(leaf * LEAF if isinstance(leaf, int) else pl.multiple_of(leaf * LEAF, LEAF), LEAF)
 
-    def direct(piece, way):
-        rows = pl.ds(2 * LEAF, 2 * LEAF) if piece == 0 else leaf_rows(way if piece == 1 else 1 - way)
+    def direct(group, way):
+        rows = pl.ds((1 - group) * 2 * LEAF, 2 * LEAF)
         return pltpu.make_async_remote_copy(
             src_ref=tok.at[rows],
             dst_ref=g.at[1 + way, rows],
             send_sem=gsend,
-            recv_sem=drecv.at[way, piece],
+            recv_sem=drecv.at[way, group],
             device_id=(t, left if way else right),
             device_id_type=MESH,
         )
@@ -121,9 +121,9 @@
             device_id_type=MESH,
         )
 
-    def send_direct(piece):
+    def send_direct(group):
         for way in range(2):
-            direct(piece, way).start()
+            direct(group, way).start()
 
     def pass_on(group):
         for way in range(2):
@@ -244,7 +244,8 @@
         scaled, _ = scaled_rows(leaf, (3,))
         inverse = part_squares[leaf]
         sums = parts[leaf, :, WIDTH:] + dot(scaled, w[3, :, WIDTH:])
-        gate[leaf_rows(leaf), :] = jax.nn.sigmoid(sums * jnp.concatenate([inverse, inverse], 1))
+        half = 0.5 * jnp.concatenate([inverse, inverse], 1)
+        gate[leaf_rows(leaf), :] = 0.5 * jnp.tanh(sums * half) + 0.5
 
     def spectrum_of(leaf):
         value = vals[leaf_rows(leaf), :]
@@ -258,7 +259,7 @@
         out_re = khat[0] * a_re - khat[1] * a_im + khat[2] * b_re - khat[3] * b_im
         out_im = khat[0] * a_im + khat[1] * a_re + khat[2] * b_im + khat[3] * b_re
         both = jnp.concatenate([out_re, out_im], 0).astype(BF16)
-        total = dot(inv_v[...], jnp.concatenate([both, both], 0))
+        total = dot(inv_v[...], both)
         near[rows, :] = total + skip_v[...] * vals[rows, :].astype(F32)
 
     def coupled(level, source_two, source_three):
@@ -320,51 +321,53 @@
 
         lax.fori_loop(first, last, step, 0)
 
+    def over(first, last, work):
+        def step(leaf, carry):
+            work(leaf)
+            return carry
+
+        lax.fori_loop(first, last, step, 0)
+
     chain(0)
     tables_near()
     send_direct(1)
     chain(1)
     tables_moments()
+    chain(2)
     tables_lift()
-    chain(2)
-
-    @pl.when(own < PLANE - 1)
-    def _():
-        pl.semaphore_wait(ready_plane, PLANE - 1 - own)
-
-    @pl.when(z < PLANES - 1)
-    def _():
-        pl.semaphore_wait(ready_next, 1)
-
-        @pl.when(y == 0)
-        def _():
-            signal(ready_edge, z * PLANE + 6, x)
-            signal(ready_edge, z * PLANE + 7, x)
-
+    chain(3)
     for slot in range(4):
         copies["v", slot].wait()
         copies["g", slot].wait()
     for name in ("tok", "gain", "skip", "coup", "inv"):
         copies[name].wait()
-    chain(3)
     pass_on(0)
-    send_direct(2)
     chain(4)
+
+    @pl.when(own < PLANE - 1)
+    def _():
+        pl.semaphore_wait(ready_plane, PLANE - 1 - own)
+
+    @pl.when(z < PLANES - 1)
+    def _():
+        pl.semaphore_wait(ready_next, 1)
+
+        @pl.when(y == 0)
+        def _():
+            signal(ready_edge, z * PLANE + 6, x)
+            signal(ready_edge, z * PLANE + 7, x)
+
     over(2, 4, gather_part)
+    chain(5)
+    tables_far()
+    inv_v[...] = inv_f[...].astype(BF16)
+    chain(6)
     pass_on(1)
-    tables_far()
-    inv_v[...] = jnp.concatenate(halves(inv_f[...]), 1)
-    chain(5)
+    over(0, 2, gather_part)
 
     @pl.when((y == 3) & (z < PLANES - 1))
     def _():
         pl.semaphore_wait(ready_edge, 2)
-
-    for way in range(2):
-        direct(2, way).wait_recv()
-    chain(6)
-    over(0, 2, gather_part)
-    chain(7)
 
     halo_copy = pltpu.make_async_remote_copy(
         src_ref=vals.at[pl.ds(3 * LEAF, LEAF)],
@@ -375,25 +378,46 @@
         device_id_type=MESH,
     )
 
-    ctx_copy = pltpu.make_async_remote_copy(
-        src_ref=ctx_out,
-        dst_ref=ctx_in,
-        send_sem=csem.at[0],
-        recv_sem=csem.at[1],
-        device_id=(t + 1, x),
-        device_id_type=MESH,
-    )
+    def ctx_copy(part):
+        rows = pl.ds(0, 48) if part == 0 else pl.ds(48, 16)
+        return pltpu.make_async_remote_copy(
+            src_ref=ctx_out.at[rows],
+            dst_ref=ctx_in.at[rows],
+            send_sem=csem.at[0, part],
+            recv_sem=csem.at[1, part],
+            device_id=(t + 1, x),
+            device_id_type=MESH,
+        )
+
+    summing = red_m[0, :RANK, :]
+
+    def gathered(level, source_two, source_three=None):
+        return dot(summing, coupled(level, source_two, source_three))
 
     wait_relayed(0)
     over(2, 4, values_of)
+    ctx_out[:48] = jnp.concatenate(
+        [moms[2, 0:16, :], moms[3, 0:16, :], moms[2, 16:32, :] + moms[3, 16:32, :]], 0
+    ).astype(BF16)
 
     @pl.when(t < PLANES * PLANE - 1)
     def _():
         halo_copy.start()
+        ctx_copy(0).start()
 
     over(2, 4, spectrum_of)
     over(2, 4, gates_of)
     near_rows(3)
+
+    @pl.when(t > 0)
+    def _():
+        ctx_copy(0).wait_recv()
+        halo_copy.wait_recv()
+
+    prev = ctx_in[:32].astype(F32)
+    far0[0] = gathered(0, prev[0:16])
+    far0[1] = gathered(0, prev[16:32], prev[0:16])
+    spec[LEAVES] = dot(fwd_v[...], jnp.concatenate([halo[...], halo[...]], 0))
 
     wait_relayed(1)
     over(0, 2, values_of)
@@ -438,25 +462,13 @@
         for target in range(2):
             next_plane_copy(target, core).start()
 
-    ctx_out[...] = jnp.concatenate(
-        [
-            moms[2, 0:16, :],
-            moms[3, 0:16, :],
-            moms[0, 16:32, :] + moms[1, 16:32, :],
-            moms[2, 16:32, :] + moms[3, 16:32, :],
-        ],
-        0,
-    ).astype(BF16)
+    ctx_out[48:] = (moms[0, 16:32, :] + moms[1, 16:32, :]).astype(BF16)
 
     @pl.when(t < PLANES * PLANE - 1)
     def _():
-        ctx_copy.start()
+        ctx_copy(1).start()
 
     over(0, 2, gates_of)
-
-    early = jnp.where(y == 0, 2, jnp.where(y == 1, 1, 0))
-    over(0, jnp.minimum(2 * early, 2), spectrum_of)
-    over(1, 1 + early, near_rows)
 
     plane_all.wait_recv()
     stack = m2[...].reshape(PLANE * RANK, WIDTH)
@@ -484,6 +496,8 @@
             device_id_type=MESH,
         )
 
+    chain(7)
+
     for k in range(PLANES - 1, 1, -1):
 
         @pl.when(z + k < PLANES)
@@ -498,33 +512,20 @@
     def _():
         pack_copy(32).start()
 
-    over(jnp.minimum(2 * early, 2), 2, spectrum_of)
-    over(1 + early, 3, near_rows)
+    over(0, 2, spectrum_of)
+    over(1, 3, near_rows)
+
+    near_rows(0)
 
     @pl.when(t > 0)
     def _():
-        halo_copy.wait_recv()
-
-    before = halo[...]
-    spec[LEAVES] = dot(fwd_v[...], jnp.concatenate([before, before], 0))
-    near_rows(0)
-
-    summing = red_m[0, :RANK, :]
-
-    def gathered(level, source_two, source_three=None):
-        return dot(summing, coupled(level, source_two, source_three))
-
-    @pl.when(t > 0)
-    def _():
-        ctx_copy.wait_recv()
-
-    prev = ctx_in[...].astype(F32)
-    far0[0] = gathered(0, prev[0:16])
-    far0[1] = gathered(0, prev[16:32], prev[0:16])
+        ctx_copy(1).wait_recv()
+
+    prev = ctx_in[32:].astype(F32)
     far0[2] = gathered(0, moms[0, 0:16, :])
     far0[3] = gathered(0, moms[1, 0:16, :], moms[0, 0:16, :])
-    far1[0] = gathered(1, prev[32:48])
-    far1[1] = gathered(1, prev[48:64], prev[32:48])
+    far1[0] = gathered(1, prev[16:32])
+    far1[1] = gathered(1, prev[0:16], prev[16:32])
 
     gather_sent = g.at[pl.ds(0, 3)]
     pltpu.make_async_remote_copy(
@@ -541,7 +542,8 @@
     @pl.when(t < PLANES * PLANE - 1)
     def _():
         halo_copy.wait_send()
-        ctx_copy.wait_send()
+        ctx_copy(0).wait_send()
+        ctx_copy(1).wait_send()
 
     @pl.when((y == 3) & (z < PLANES - 1))
     def _():
@@ -669,7 +671,7 @@
         vmem(forward.shape, F32),
         vmem(inverse.shape, F32),
         vmem((2 * LEAF, 2 * LEAF), BF16),
-        vmem((LEAF, 4 * LEAF), BF16),
+        vmem((LEAF, 2 * LEAF), BF16),
         vmem((frames, WIDTH), BF16),
         vmem((LEAF, WIDTH), BF16),
         vmem((frames, WIDTH), F32),
@@ -696,10 +698,10 @@
         vmem((LEAVES, LEAF, WIDTH // 2), F32),
         dma((20,)),
         dma(()),
-        dma((2, 3)),
+        dma((2, 2)),
         dma((2, 2)),
         dma((2,)),
-        dma((2,)),
+        dma((2, 2)),
         dma(()),
         dma(()),
         dma((2,)),

time: 35.9 us -> 36.2 us (level)
  the two profiles are of different devices: /device:TPU:224 before, /device:TPU:200 now
where the time goes in v3:
time: 36.2 us; the launch traced here: 36.1 us
  Pallas kernels  34.2 us (94%)
  local copies, waits for them, and re-layouts  1.87 us (5%)
    pallas_call x1, Pallas kernels, per_device(): pl.pallas_call(body, out_shape=jax.ShapeDtypeStruct(tokens.shape, BF16),...  34.2 us
    unnamed x1, local copies, waits for them, and re-layouts  1.87 us

profile of v3, /device:TPU:200, one launch (start us, length us, event | category | flops | bytes accessed | tf_op | source)
XLA Modules:
  0.0 36.1 jit_solution(16724763441260519307)
XLA Ops:
  0.0 34.2 %shard_map.136 = bf16[1024,256]{1,0:T(8,128)(2,1)} custom-call(bf16[1024,256]{1,0:T(8,128)(2,1)} %tok.1, f32[1,1024]{1,0:T(1,128)} %bitcast.2, bf16[1024,256]{1,0:T(8,128)(2,1)} %w_value.1, bf16[1024,256]{1,0:T(8,128)(2,1)} %w_gate.1, f32[32,512]{1,0:T(8,128)} %phi.1, f32[32,256]{1,0:T(8,128)} %coeff.1, f32[1,256]{1,0:T(1,128)} %bitcast.3, f32[16,256]{1,0:T(8,128)} %up.1, ...), custom_call_target="tpu_custom_call" | custom-call | flops 4000000000 | bytes 8000000 | tf_op jit(solution)/shard_map/pallas_call | solution.py:719
  34.2 1.9 %copy.16 = bf16[1024,256]{1,0:T(8,128)(2,1)} copy(bf16[1024,256]{1,0:T(8,128)(2,1)} %shard_map.136) | data formatting | bytes 1048576

commit v4 on v3

--- a/solution.py
+++ b/solution.py
@@ -215,9 +215,12 @@
             lane_at = lax.broadcasted_iota(jnp.int32, whole.shape, 1)
             far_m[leaf] = jnp.where(lane_at < 96, high, whole - high).astype(BF16)
 
-    def scaled_rows(leaf, slots):
-        rows = leaf_rows(leaf)
-        squares = jnp.zeros((LEAF, WIDTH), F32)
+    def pair_rows(first):
+        return pl.ds(first * LEAF, 2 * LEAF)
+
+    def scaled_rows(first, slots):
+        rows = pair_rows(first)
+        squares = jnp.zeros((2 * LEAF, WIDTH), F32)
         columns = []
         for slot in slots:
             tokens = g[slot, rows, :].astype(F32)
@@ -226,41 +229,50 @@
             columns.append((tokens * scale).astype(BF16))
         return jnp.concatenate(columns, 1), squares
 
-    def gather_part(leaf):
-        scaled, squares = scaled_rows(leaf, (0, 1, 2))
-        parts[leaf] = dot(scaled, w[:3].reshape(3 * WIDTH, 2 * WIDTH))
-        part_squares[leaf] = squares[:, : WIDTH // 2] + squares[:, WIDTH // 2 :]
-
-    def values_of(leaf):
-        scaled, squares = scaled_rows(leaf, (3,))
-        squares = squares[:, : WIDTH // 2] + squares[:, WIDTH // 2 :] + part_squares[leaf]
+    def gather_pair(first):
+        scaled, squares = scaled_rows(first, (0, 1, 2))
+        parts[pair_rows(first), :] = dot(scaled, w[:3].reshape(3 * WIDTH, 2 * WIDTH))
+        part_squares[pair_rows(first), :] = squares[:, : WIDTH // 2] + squares[:, WIDTH // 2 :]
+
+    def values_of(first):
+        rows = pair_rows(first)
+        scaled, squares = scaled_rows(first, (3,))
+        squares = squares[:, : WIDTH // 2] + squares[:, WIDTH // 2 :] + part_squares[rows, :]
         inverse = lax.rsqrt(jnp.sum(squares, axis=1, keepdims=True) / 1024 + 1e-06)
-        part_squares[leaf] = jnp.broadcast_to(inverse, squares.shape)
-        value = ((parts[leaf, :, :WIDTH] + dot(scaled, w[3, :, :WIDTH])) * inverse).astype(BF16)
-        vals[leaf_rows(leaf), :] = value
-        moms[leaf] = dot(mom_m[leaf], jnp.concatenate([value, value], 0))
-
-    def gates_of(leaf):
-        scaled, _ = scaled_rows(leaf, (3,))
-        inverse = part_squares[leaf]
-        sums = parts[leaf, :, WIDTH:] + dot(scaled, w[3, :, WIDTH:])
-        half = 0.5 * jnp.concatenate([inverse, inverse], 1)
-        gate[leaf_rows(leaf), :] = 0.5 * jnp.tanh(sums * half) + 0.5
-
-    def spectrum_of(leaf):
-        value = vals[leaf_rows(leaf), :]
-        spec[leaf] = dot(fwd_v[...], jnp.concatenate([value, value], 0))
-
-    def near_rows(leaf):
-        rows = leaf_rows(leaf)
-        before = (leaf - 1 if leaf > 0 else LEAVES) if isinstance(leaf, int) else leaf - 1
-        a_re, a_im = spec[leaf, :LEAF, :], spec[leaf, LEAF:, :]
-        b_re, b_im = spec[before, :LEAF, :], spec[before, LEAF:, :]
-        out_re = khat[0] * a_re - khat[1] * a_im + khat[2] * b_re - khat[3] * b_im
-        out_im = khat[0] * a_im + khat[1] * a_re + khat[2] * b_im + khat[3] * b_re
-        both = jnp.concatenate([out_re, out_im], 0).astype(BF16)
-        total = dot(inv_v[...], both)
-        near[rows, :] = total + skip_v[...] * vals[rows, :].astype(F32)
+        part_squares[rows, :] = jnp.broadcast_to(inverse, squares.shape)
+        value = ((parts[rows, :WIDTH] + dot(scaled, w[3, :, :WIDTH])) * inverse).astype(BF16)
+        vals[rows, :] = value
+        for k in range(2):
+            leaf_value = value[k * LEAF : (k + 1) * LEAF]
+            moms[first + k] = dot(mom_m[first + k], jnp.concatenate([leaf_value, leaf_value], 0))
+
+    def gates_of(first):
+        rows = pair_rows(first)
+        scaled, _ = scaled_rows(first, (3,))
+        half = 0.5 * part_squares[rows, :]
+        sums = parts[rows, WIDTH:] + dot(scaled, w[3, :, WIDTH:])
+        gate[rows, :] = 0.5 * jnp.tanh(sums * jnp.concatenate([half, half], 1)) + 0.5
+
+    def spectra(first):
+        both = jnp.concatenate([vals[leaf_rows(first), :], vals[leaf_rows(first + 1), :]], 1)
+        result = dot(fwd_v[...], jnp.concatenate([both, both], 0))
+        spec[first] = result[:, :WIDTH]
+        spec[first + 1] = result[:, WIDTH:]
+
+    def near_rows(leaves):
+        columns = []
+        for leaf in leaves:
+            before = leaf - 1 if leaf > 0 else LEAVES
+            a_re, a_im = spec[leaf, :LEAF, :], spec[leaf, LEAF:, :]
+            b_re, b_im = spec[before, :LEAF, :], spec[before, LEAF:, :]
+            out_re = khat[0] * a_re - khat[1] * a_im + khat[2] * b_re - khat[3] * b_im
+            out_im = khat[0] * a_im + khat[1] * a_re + khat[2] * b_im + khat[3] * b_re
+            columns.append(jnp.concatenate([out_re, out_im], 0).astype(BF16))
+        total = dot(inv_v[...], jnp.concatenate(columns, 1))
+        for k, leaf in enumerate(leaves):
+            rows = leaf_rows(leaf)
+            direct_term = skip_v[...] * vals[rows, :].astype(F32)
+            near[rows, :] = total[:, k * WIDTH : (k + 1) * WIDTH] + direct_term
 
     def coupled(level, source_two, source_three):
         product = coup_v[level, 0] * source_two[None]
@@ -314,20 +326,6 @@
             if not isinstance(place, int) or place < PLANES - 1:
                 signal(ready_later, t - PLANE, x)
 
-    def over(first, last, work):
-        def step(leaf, carry):
-            work(leaf)
-            return carry
-
-        lax.fori_loop(first, last, step, 0)
-
-    def over(first, last, work):
-        def step(leaf, carry):
-            work(leaf)
-            return carry
-
-        lax.fori_loop(first, last, step, 0)
-
     chain(0)
     tables_near()
     send_direct(1)
@@ -357,13 +355,13 @@
             signal(ready_edge, z * PLANE + 6, x)
             signal(ready_edge, z * PLANE + 7, x)
 
-    over(2, 4, gather_part)
+    gather_pair(2)
     chain(5)
     tables_far()
     inv_v[...] = inv_f[...].astype(BF16)
     chain(6)
     pass_on(1)
-    over(0, 2, gather_part)
+    gather_pair(0)
 
     @pl.when((y == 3) & (z < PLANES - 1))
     def _():
@@ -395,7 +393,7 @@
         return dot(summing, coupled(level, source_two, source_three))
 
     wait_relayed(0)
-    over(2, 4, values_of)
+    values_of(2)
     ctx_out[:48] = jnp.concatenate(
         [moms[2, 0:16, :], moms[3, 0:16, :], moms[2, 16:32, :] + moms[3, 16:32, :]], 0
     ).astype(BF16)
@@ -405,22 +403,12 @@
         halo_copy.start()
         ctx_copy(0).start()
 
-    over(2, 4, spectrum_of)
-    over(2, 4, gates_of)
-    near_rows(3)
-
-    @pl.when(t > 0)
-    def _():
-        ctx_copy(0).wait_recv()
-        halo_copy.wait_recv()
-
-    prev = ctx_in[:32].astype(F32)
-    far0[0] = gathered(0, prev[0:16])
-    far0[1] = gathered(0, prev[16:32], prev[0:16])
-    spec[LEAVES] = dot(fwd_v[...], jnp.concatenate([halo[...], halo[...]], 0))
+    spectra(2)
+    gates_of(2)
+    near_rows((3,))
 
     wait_relayed(1)
-    over(0, 2, values_of)
+    values_of(0)
 
     total = moms[0, 32:48, :] + moms[1, 32:48, :] + moms[2, 32:48, :] + moms[3, 32:48, :]
     m2[own] = total.astype(BF16)
@@ -468,7 +456,7 @@
     def _():
         ctx_copy(1).start()
 
-    over(0, 2, gates_of)
+    gates_of(0)
 
     plane_all.wait_recv()
     stack = m2[...].reshape(PLANE * RANK, WIDTH)
@@ -512,20 +500,27 @@
     def _():
         pack_copy(32).start()
 
-    over(0, 2, spectrum_of)
-    over(1, 3, near_rows)
-
-    near_rows(0)
+    spectra(0)
 
     @pl.when(t > 0)
     def _():
+        halo_copy.wait_recv()
+
+    spec[LEAVES] = dot(fwd_v[...], jnp.concatenate([halo[...], halo[...]], 0))
+    near_rows((0, 1, 2))
+
+    @pl.when(t > 0)
+    def _():
+        ctx_copy(0).wait_recv()
         ctx_copy(1).wait_recv()
 
-    prev = ctx_in[32:].astype(F32)
+    prev = ctx_in[...].astype(F32)
+    far0[0] = gathered(0, prev[0:16])
+    far0[1] = gathered(0, prev[16:32], prev[0:16])
     far0[2] = gathered(0, moms[0, 0:16, :])
     far0[3] = gathered(0, moms[1, 0:16, :], moms[0, 0:16, :])
-    far1[0] = gathered(1, prev[16:32])
-    far1[1] = gathered(1, prev[0:16], prev[16:32])
+    far1[0] = gathered(1, prev[48:64])
+    far1[1] = gathered(1, prev[32:48], prev[48:64])
 
     gather_sent = g.at[pl.ds(0, 3)]
     pltpu.make_async_remote_copy(
@@ -694,8 +689,8 @@
         vmem((LEAVES, RANK, WIDTH), F32),
         vmem((2, RANK, WIDTH), F32),
         vmem((frames, WIDTH), BF16),
-        vmem((LEAVES, LEAF, 2 * WIDTH), F32),
-        vmem((LEAVES, LEAF, WIDTH // 2), F32),
+        vmem((frames, 2 * WIDTH), F32),
+        vmem((frames, WIDTH // 2), F32),
         dma((20,)),
         dma(()),
         dma((2, 2)),

time: 36.2 us -> 34.9 us (0.964)
  the two profiles are of different devices: /device:TPU:200 before, /device:TPU:224 now
where the time goes in v4:
time: 34.9 us; the launch traced here: 34.8 us
  Pallas kernels  32.9 us (94%)
  local copies, waits for them, and re-layouts  1.87 us (5%)
    pallas_call x1, Pallas kernels, per_device(): pl.pallas_call(body, out_shape=jax.ShapeDtypeStruct(tokens.shape, BF16),...  32.9 us
    unnamed x1, local copies, waits for them, and re-layouts  1.87 us

profile of v4, /device:TPU:224, one launch (start us, length us, event | category | flops | bytes accessed | tf_op | source)
XLA Modules:
  0.0 34.8 jit_solution(18387020209349256336)
XLA Ops:
  0.0 32.9 %shard_map.136 = bf16[1024,256]{1,0:T(8,128)(2,1)} custom-call(bf16[1024,256]{1,0:T(8,128)(2,1)} %tok.1, f32[1,1024]{1,0:T(1,128)} %bitcast.2, bf16[1024,256]{1,0:T(8,128)(2,1)} %w_value.1, bf16[1024,256]{1,0:T(8,128)(2,1)} %w_gate.1, f32[32,512]{1,0:T(8,128)} %phi.1, f32[32,256]{1,0:T(8,128)} %coeff.1, f32[1,256]{1,0:T(1,128)} %bitcast.3, f32[16,256]{1,0:T(8,128)} %up.1, ...), custom_call_target="tpu_custom_call" | custom-call | flops 4000000000 | bytes 8000000 | tf_op jit(solution)/shard_map/pallas_call | solution.py:714
  32.9 1.9 %copy.16 = bf16[1024,256]{1,0:T(8,128)(2,1)} copy(bf16[1024,256]{1,0:T(8,128)(2,1)} %shard_map.136) | data formatting | bytes 1048576

commit v5 on v4

--- a/solution.py
+++ b/solution.py
@@ -125,9 +125,12 @@
         for way in range(2):
             direct(group, way).start()
 
+    def arrive(group):
+        for way in range(2):
+            direct(group, way).wait_recv()
+
     def pass_on(group):
         for way in range(2):
-            direct(group, way).wait_recv()
             relay(group, way).start()
 
     def wait_relayed(group):
@@ -281,6 +284,7 @@
         return product.reshape(RANK * RANK, WIDTH).astype(BF16)
 
     send_direct(0)
+    send_direct(1)
 
     copies = {}
 
@@ -328,18 +332,18 @@
 
     chain(0)
     tables_near()
-    send_direct(1)
     chain(1)
     tables_moments()
     chain(2)
     tables_lift()
     chain(3)
+    tables_far()
+    for name in ("tok", "gain", "skip", "coup", "inv"):
+        copies[name].wait()
+    inv_v[...] = inv_f[...].astype(BF16)
     for slot in range(4):
         copies["v", slot].wait()
         copies["g", slot].wait()
-    for name in ("tok", "gain", "skip", "coup", "inv"):
-        copies[name].wait()
-    pass_on(0)
     chain(4)
 
     @pl.when(own < PLANE - 1)
@@ -355,13 +359,14 @@
             signal(ready_edge, z * PLANE + 6, x)
             signal(ready_edge, z * PLANE + 7, x)
 
+    chain(5)
+    arrive(0)
+    pass_on(0)
     gather_pair(2)
-    chain(5)
-    tables_far()
-    inv_v[...] = inv_f[...].astype(BF16)
     chain(6)
+    arrive(1)
+    gather_pair(0)
     pass_on(1)
-    gather_pair(0)
 
     @pl.when((y == 3) & (z < PLANES - 1))
     def _():
@@ -458,6 +463,16 @@
 
     gates_of(0)
 
+    def own_work():
+        spectra(0)
+        near_rows((1, 2))
+        far0[2] = gathered(0, moms[0, 0:16, :])
+        far0[3] = gathered(0, moms[1, 0:16, :], moms[0, 0:16, :])
+
+    @pl.when(y == 0)
+    def _():
+        own_work()
+
     plane_all.wait_recv()
     stack = m2[...].reshape(PLANE * RANK, WIDTH)
     lifted = dot(lift_m[...], jnp.concatenate([stack, stack], 0))
@@ -500,14 +515,16 @@
     def _():
         pack_copy(32).start()
 
-    spectra(0)
+    @pl.when(y > 0)
+    def _():
+        own_work()
 
     @pl.when(t > 0)
     def _():
         halo_copy.wait_recv()
 
     spec[LEAVES] = dot(fwd_v[...], jnp.concatenate([halo[...], halo[...]], 0))
-    near_rows((0, 1, 2))
+    near_rows((0,))
 
     @pl.when(t > 0)
     def _():
@@ -517,8 +534,6 @@
     prev = ctx_in[...].astype(F32)
     far0[0] = gathered(0, prev[0:16])
     far0[1] = gathered(0, prev[16:32], prev[0:16])
-    far0[2] = gathered(0, moms[0, 0:16, :])
-    far0[3] = gathered(0, moms[1, 0:16, :], moms[0, 0:16, :])
     far1[0] = gathered(1, prev[48:64])
     far1[1] = gathered(1, prev[32:48], prev[48:64])
 

time: 34.9 us -> 35.7 us (1.023)
  Pallas kernels: 32.9 us -> 33.7 us
    pallas_call x1, Pallas kernels: 32.9 us -> 33.7 us  [per_device(): pl.pallas_call(body, out_shape=jax.ShapeDtypeStruct(tokens.shape, BF16),...]
where the time goes in v5:
time: 35.7 us; the launch traced here: 35.6 us
  Pallas kernels  33.7 us (94%)
  local copies, waits for them, and re-layouts  1.87 us (5%)
    pallas_call x1, Pallas kernels, per_device(): pl.pallas_call(body, out_shape=jax.ShapeDtypeStruct(tokens.shape, BF16),...  33.7 us
    unnamed x1, local copies, waits for them, and re-layouts  1.87 us

profile of v5, /device:TPU:224, one launch (start us, length us, event | category | flops | bytes accessed | tf_op | source)
XLA Modules:
  0.0 35.6 jit_solution(3608773280710113511)
XLA Ops:
  0.0 33.7 %shard_map.136 = bf16[1024,256]{1,0:T(8,128)(2,1)} custom-call(bf16[1024,256]{1,0:T(8,128)(2,1)} %tok.1, f32[1,1024]{1,0:T(1,128)} %bitcast.2, bf16[1024,256]{1,0:T(8,128)(2,1)} %w_value.1, bf16[1024,256]{1,0:T(8,128)(2,1)} %w_gate.1, f32[32,512]{1,0:T(8,128)} %phi.1, f32[32,256]{1,0:T(8,128)} %coeff.1, f32[1,256]{1,0:T(1,128)} %bitcast.3, f32[16,256]{1,0:T(8,128)} %up.1, ...), custom_call_target="tpu_custom_call" | custom-call | flops 4000000000 | bytes 8000000 | tf_op jit(solution)/shard_map/pallas_call | solution.py:729
  33.7 1.9 %copy.16 = bf16[1024,256]{1,0:T(8,128)(2,1)} copy(bf16[1024,256]{1,0:T(8,128)(2,1)} %shard_map.136) | data formatting | bytes 1048576

commit v6 on v4

--- a/solution.py
+++ b/solution.py
@@ -54,10 +54,10 @@
 
 def body(
     tok, gain, w_value, w_gate, phi, coeff, skip, up, down, lift, spread, coup, fwd, inv,
-    out,
+    gate_out, near_out, far_out, expansion_out,
     g, w, gain_v, phi_v, coeff_v, skip_v, up_v, down_v, lift_v, spread_v, coup_v, fwd_f, inv_f, fwd_v, inv_v,
     vals, halo, gate, near, spec, khat, mom_m, lift_m, six_m, far_m, red_m, moms,
-    m2, m2_prev, ctx_out, ctx_in, pack_out, pack_in, m5_in, far0, far1, out_v, parts, part_squares,
+    m2, m2_prev, ctx_out, ctx_in, pack_out, pack_in, m5_in, expansions, parts, part_squares,
     local_sem, gsend, drecv, rrecv, hsem, csem, s1, r1, s1p, r1p, s2, r2, s5, r5, ready_plane, ready_next, ready_edge, ready_later, osem,
 ):
     t = lax.axis_index("tm")
@@ -98,6 +98,9 @@
 
     def leaf_rows(leaf):
         return pl.ds(leaf * LEAF if isinstance(leaf, int) else pl.multiple_of(leaf * LEAF, LEAF), LEAF)
+
+    def pair_rows(first):
+        return pl.ds(first * LEAF, 2 * LEAF)
 
     def direct(group, way):
         rows = pl.ds((1 - group) * 2 * LEAF, 2 * LEAF)
@@ -133,6 +136,18 @@
     def wait_relayed(group):
         for way in range(2):
             relay(group, way).wait_recv()
+
+    def handed(part):
+        source, target = (
+            (far_m, far_out),
+            (gate.at[pair_rows(2)], gate_out.at[pair_rows(2)]),
+            (gate.at[pair_rows(0)], gate_out.at[pair_rows(0)]),
+            (near.at[leaf_rows(3)], near_out.at[leaf_rows(3)]),
+            (near.at[pl.ds(0, 3 * LEAF)], near_out.at[pl.ds(0, 3 * LEAF)]),
+            (expansions.at[pl.ds(0, 6)], expansion_out.at[pl.ds(0, 6)]),
+            (expansions.at[pl.ds(6, 1)], expansion_out.at[pl.ds(6, 1)]),
+        )[part]
+        return pltpu.make_async_copy(source, target, osem.at[part])
 
     def tables_near():
         for name in ("phi", "coeff", "fwd"):
@@ -215,9 +230,6 @@
             lane_at = lax.broadcasted_iota(jnp.int32, whole.shape, 1)
             far_m[leaf] = jnp.where(lane_at < 96, high, whole - high).astype(BF16)
 
-    def pair_rows(first):
-        return pl.ds(first * LEAF, 2 * LEAF)
-
     def scaled_rows(first, slots):
         rows = pair_rows(first)
         squares = jnp.zeros((2 * LEAF, WIDTH), F32)
@@ -251,7 +263,7 @@
         scaled, _ = scaled_rows(first, (3,))
         half = 0.5 * part_squares[rows, :]
         sums = parts[rows, WIDTH:] + dot(scaled, w[3, :, WIDTH:])
-        gate[rows, :] = 0.5 * jnp.tanh(sums * jnp.concatenate([half, half], 1)) + 0.5
+        gate[rows, :] = (0.5 * jnp.tanh(sums * jnp.concatenate([half, half], 1)) + 0.5).astype(BF16)
 
     def spectra(first):
         both = jnp.concatenate([vals[leaf_rows(first), :], vals[leaf_rows(first + 1), :]], 1)
@@ -272,7 +284,7 @@
         for k, leaf in enumerate(leaves):
             rows = leaf_rows(leaf)
             direct_term = skip_v[...] * vals[rows, :].astype(F32)
-            near[rows, :] = total[:, k * WIDTH : (k + 1) * WIDTH] + direct_term
+            near[rows, :] = (total[:, k * WIDTH : (k + 1) * WIDTH] + direct_term).astype(BF16)
 
     def coupled(level, source_two, source_three):
         product = coup_v[level, 0] * source_two[None]
@@ -358,6 +370,7 @@
     gather_pair(2)
     chain(5)
     tables_far()
+    handed(0).start()
     inv_v[...] = inv_f[...].astype(BF16)
     chain(6)
     pass_on(1)
@@ -405,7 +418,9 @@
 
     spectra(2)
     gates_of(2)
+    handed(1).start()
     near_rows((3,))
+    handed(3).start()
 
     wait_relayed(1)
     values_of(0)
@@ -457,6 +472,7 @@
         ctx_copy(1).start()
 
     gates_of(0)
+    handed(2).start()
 
     plane_all.wait_recv()
     stack = m2[...].reshape(PLANE * RANK, WIDTH)
@@ -508,6 +524,7 @@
 
     spec[LEAVES] = dot(fwd_v[...], jnp.concatenate([halo[...], halo[...]], 0))
     near_rows((0, 1, 2))
+    handed(4).start()
 
     @pl.when(t > 0)
     def _():
@@ -515,12 +532,13 @@
         ctx_copy(1).wait_recv()
 
     prev = ctx_in[...].astype(F32)
-    far0[0] = gathered(0, prev[0:16])
-    far0[1] = gathered(0, prev[16:32], prev[0:16])
-    far0[2] = gathered(0, moms[0, 0:16, :])
-    far0[3] = gathered(0, moms[1, 0:16, :], moms[0, 0:16, :])
-    far1[0] = gathered(1, prev[48:64])
-    far1[1] = gathered(1, prev[32:48], prev[48:64])
+    expansions[0] = gathered(0, prev[0:16])
+    expansions[1] = gathered(0, prev[16:32], prev[0:16])
+    expansions[2] = gathered(0, moms[0, 0:16, :])
+    expansions[3] = gathered(0, moms[1, 0:16, :], moms[0, 0:16, :])
+    expansions[4] = gathered(1, prev[48:64])
+    expansions[5] = gathered(1, prev[32:48], prev[48:64])
+    handed(5).start()
 
     gather_sent = g.at[pl.ds(0, 3)]
     pltpu.make_async_remote_copy(
@@ -600,19 +618,8 @@
         4, sixth(4 + odd), sixth(6 + odd) * odd_six.astype(F32)
     )
 
-    expansion = expansion[:RANK] + expansion[RANK:]
-
-    def out_copy(leaf):
-        rows = leaf_rows(leaf)
-        return pltpu.make_async_copy(out_v.at[rows], out.at[rows], osem.at[leaf])
-
-    for leaf in range(LEAVES):
-        rows = leaf_rows(leaf)
-        high, low = halves(jnp.concatenate([far0[leaf], far1[leaf // 2], expansion], 0))
-        whole = jnp.concatenate([high, low, high, jnp.zeros((112, WIDTH), BF16)], 0)
-        combined = near[rows, :] + dot(far_m[leaf], whole)
-        out_v[rows, :] = (gate[rows, :] * combined).astype(BF16)
-        out_copy(leaf).start()
+    expansions[6] = expansion[:RANK] + expansion[RANK:]
+    handed(6).start()
 
     @pl.when((z < PLANES - 1) & (y < 2))
     def _():
@@ -628,8 +635,41 @@
         def _():
             five_copy(k).wait_send()
 
+    for part in range(7):
+        handed(part).wait()
+
+
+def finish(gate, near, far, expansions, out, gate_v, near_v, far_v, expansions_v, out_v, sems):
+    def rows_of(leaf):
+        return pl.ds(leaf * LEAF, LEAF)
+
+    incoming = [
+        pltpu.make_async_copy(expansions, expansions_v, sems.at[0]),
+        pltpu.make_async_copy(far, far_v, sems.at[1]),
+    ]
     for leaf in range(LEAVES):
-        out_copy(leaf).wait()
+        rows = rows_of(leaf)
+        incoming.append(pltpu.make_async_copy(near.at[rows], near_v.at[rows], sems.at[2 + 2 * leaf]))
+        incoming.append(pltpu.make_async_copy(gate.at[rows], gate_v.at[rows], sems.at[3 + 2 * leaf]))
+    for copy in incoming:
+        copy.start()
+    incoming[0].wait()
+    incoming[1].wait()
+    outgoing = []
+    for leaf in range(LEAVES):
+        rows = rows_of(leaf)
+        stack = jnp.concatenate([expansions_v[leaf], expansions_v[4 + leaf // 2], expansions_v[6]], 0)
+        high, low = halves(stack)
+        whole = jnp.concatenate([high, low, high, jnp.zeros((112, WIDTH), BF16)], 0)
+        far_rows = dot(far_v[leaf], whole)
+        incoming[2 + 2 * leaf].wait()
+        incoming[3 + 2 * leaf].wait()
+        combined = near_v[rows, :].astype(F32) + far_rows
+        out_v[rows, :] = (gate_v[rows, :].astype(F32) * combined).astype(BF16)
+        outgoing.append(pltpu.make_async_copy(out_v.at[rows], out.at[rows], sems.at[10 + leaf]))
+        outgoing[leaf].start()
+    for copy in outgoing:
+        copy.wait()
 
 
 def per_device(
@@ -669,8 +709,8 @@
         vmem((LEAF, 2 * LEAF), BF16),
         vmem((frames, WIDTH), BF16),
         vmem((LEAF, WIDTH), BF16),
-        vmem((frames, WIDTH), F32),
-        vmem((frames, WIDTH), F32),
+        vmem((frames, WIDTH), BF16),
+        vmem((frames, WIDTH), BF16),
         vmem((LEAVES + 1, 2 * LEAF, WIDTH), F32),
         vmem((4, LEAF, WIDTH), F32),
         vmem((LEAVES, 48, 2 * LEAF), BF16),
@@ -686,9 +726,7 @@
         vmem((80, WIDTH), BF16),
         vmem((64, WIDTH), BF16),
         vmem((PLANES, RANK, WIDTH), BF16),
-        vmem((LEAVES, RANK, WIDTH), F32),
-        vmem((2, RANK, WIDTH), F32),
-        vmem((frames, WIDTH), BF16),
+        vmem((7, RANK, WIDTH), F32),
         vmem((frames, 2 * WIDTH), F32),
         vmem((frames, WIDTH // 2), F32),
         dma((20,)),
@@ -709,13 +747,19 @@
         pltpu.SemaphoreType.REGULAR,
         pltpu.SemaphoreType.REGULAR,
         pltpu.SemaphoreType.REGULAR,
-        dma((LEAVES,)),
+        dma((7,)),
     ]
-    return pl.pallas_call(
+    handed = [
+        jax.ShapeDtypeStruct((frames, WIDTH), BF16),
+        jax.ShapeDtypeStruct((frames, WIDTH), BF16),
+        jax.ShapeDtypeStruct((LEAVES, LEAF, LEAF), BF16),
+        jax.ShapeDtypeStruct((7, RANK, WIDTH), F32),
+    ]
+    results = pl.pallas_call(
         body,
-        out_shape=jax.ShapeDtypeStruct(tokens.shape, BF16),
+        out_shape=handed,
         in_specs=[in_hbm] * 14,
-        out_specs=in_hbm,
+        out_specs=[in_hbm] * 4,
         scratch_shapes=scratch,
         compiler_params=pltpu.CompilerParams(
             collective_id=0, has_side_effects=True, vmem_limit_bytes=60 * 1024 * 1024
@@ -737,6 +781,16 @@
         jnp.asarray(forward),
         jnp.asarray(inverse),
     )
+    return pl.pallas_call(
+        finish,
+        out_shape=jax.ShapeDtypeStruct(tokens.shape, BF16),
+        in_specs=[in_hbm] * 4,
+        out_specs=in_hbm,
+        scratch_shapes=[vmem(item.shape, item.dtype) for item in handed]
+        + [vmem((frames, WIDTH), BF16), dma((10 + LEAVES,))],
+        compiler_params=pltpu.CompilerParams(vmem_limit_bytes=60 * 1024 * 1024),
+        cost_estimate=pl.CostEstimate(flops=2 * 10**8, bytes_accessed=2 * 10**6, transcendentals=0),
+    )(*results)
 
 
 def solution(mesh):

time: 34.9 us -> 35.3 us (1.011)
  Pallas kernels: 32.9 us -> 35.2 us
  local copies, waits for them, and re-layouts: 1.87 us -> 0 us
    pallas_call x1 -> x2, Pallas kernels: 32.9 us -> 35.2 us  [the longest x1 32.5 us: per_device(): pl.pallas_call(body, out_shape=handed, in_specs=[in_hbm] * 14, out_specs=...]
    unnamed x1 -> x0, local copies, waits for them, and re-layouts: 1.87 us -> none
where the time goes in v6:
time: 35.3 us; the launch traced here: 35.2 us
  Pallas kernels  35.2 us (100%)
    pallas_call x1, Pallas kernels, per_device(): pl.pallas_call(body, out_shape=handed, in_specs=[in_hbm] * 14, out_specs=...  32.5 us
    pallas_call x1, Pallas kernels, per_device(): pl.pallas_call(finish, out_shape=jax.ShapeDtypeStruct(tokens.shape, BF16)...  2.74 us

profile of v6, /device:TPU:224, one launch (start us, length us, event | category | flops | bytes accessed | tf_op | source)
XLA Modules:
  0.0 35.2 jit_solution(16155443720514671184)
XLA Ops:
  0.0 32.5 %shard_map.136 = (bf16[1024,256]{1,0:T(8,128)(2,1)}, bf16[1024,256]{1,0:T(8,128)(2,1)}, bf16[4,256,256]{2,1,0:T(8,128)(2,1)}, f32[7,16,256]{2,1,0:T(8,128)}) custom-call(bf16[1024,256]{1,0:T(8,128)(2,1)} %tok.1, f32[1,1024]{1,0:T(1,128)} %bitcast.2, bf16[1024,256]{1,0:T(8,128)(2,1)} %w_value.1, bf16[1024,256]{1,0:T(8,128)(2,1)} %w_gate.1, f32[32,512]{1,0:T(8,128)} %phi.1, ...), custom_call_target="tpu_custom_call" | custom-call | flops 4000000000 | bytes 8000000 | tf_op jit(solution)/shard_map/pallas_call | solution.py:758
  32.5 2.7 %shard_map.137 = bf16[1024,256]{1,0:T(8,128)(2,1)} custom-call(bf16[1024,256]{1,0:T(8,128)(2,1)} %get-tuple-element.9.gate, bf16[1024,256]{1,0:T(8,128)(2,1)} %get-tuple-element.10.near, bf16[4,256,256]{2,1,0:T(8,128)(2,1)} %get-tuple-element.11.far, f32[7,16,256]{2,1,0:T(8,128)} %get-tuple-element.12.expansions), custom_call_target="tpu_custom_call" | custom-call | flops 200000000 | bytes 2000000 | tf_op jit(solution)/shard_map/pallas_call | solution.py:784

commit v7 on v4

--- a/solution.py
+++ b/solution.py
@@ -66,6 +66,7 @@
     y = lax.rem(lax.div(t, 2), 4)
     z = lax.div(t, PLANE)
     own = lax.rem(t, PLANE)
+    rank = 2 * y + 1 - core
     right, left = lax.rem(x + 1, 4), lax.rem(x + 3, 4)
 
     barrier = pltpu.get_barrier_semaphore()
@@ -79,12 +80,6 @@
     @pl.when(z < PLANES - 1)
     def _():
         signal(barrier, t + PLANE, x)
-
-    for k in range(1, PLANE):
-
-        @pl.when(own + k < PLANE)
-        def _():
-            signal(barrier, t + k, x)
 
     m2_prev[...] = jnp.zeros_like(m2_prev)
     ctx_in[...] = jnp.zeros_like(ctx_in)
@@ -92,7 +87,16 @@
     m5_in[...] = jnp.zeros_like(m5_in)
     halo[...] = jnp.zeros_like(halo)
 
-    pl.semaphore_wait(barrier, 2 + own + jnp.where(z > 0, 1, 0))
+    def at_rank(other):
+        return z * PLANE + 2 * lax.div(other, 2) + 1 - lax.rem(other, 2)
+
+    for k in range(1, PLANE):
+
+        @pl.when(rank + k < PLANE)
+        def _():
+            signal(barrier, at_rank(rank + k), x)
+
+    pl.semaphore_wait(barrier, 2 + rank + jnp.where(z > 0, 1, 0))
 
     owners = [x, left, right, lax.rem(x + 2, 4)]
 
@@ -314,9 +318,9 @@
 
     for k in range(1, PLANE):
 
-        @pl.when(own >= k)
+        @pl.when(rank >= k)
         def _():
-            signal(ready_plane, t - k, x)
+            signal(ready_plane, at_rank(rank - k), x)
 
     def chain(place):
         @pl.when(z == PLANES - 1 - place)
@@ -342,9 +346,9 @@
     pass_on(0)
     chain(4)
 
-    @pl.when(own < PLANE - 1)
-    def _():
-        pl.semaphore_wait(ready_plane, PLANE - 1 - own)
+    @pl.when(rank < PLANE - 1)
+    def _():
+        pl.semaphore_wait(ready_plane, PLANE - 1 - rank)
 
     @pl.when(z < PLANES - 1)
     def _():
@@ -492,7 +496,11 @@
         def _():
             five_copy(k).start()
 
-    @pl.when((z < PLANES - 1) & (y < 2))
+    @pl.when((z < PLANES - 1) & (y == 0))
+    def _():
+        pack_copy(48).start()
+
+    @pl.when((z < PLANES - 1) & (y == 1))
     def _():
         pack_copy(64).start()
 
@@ -559,7 +567,11 @@
     three = jnp.where(inside, m2[at], m2_prev[0]).astype(F32) * core.astype(F32)
     expansion = reduced(0, two, three)
 
-    @pl.when((z > 0) & (y < 2))
+    @pl.when((z > 0) & (y == 0))
+    def _():
+        pack_copy(48).wait_recv()
+
+    @pl.when((z > 0) & (y == 1))
     def _():
         pack_copy(64).wait_recv()
 
@@ -614,7 +626,11 @@
         out_v[rows, :] = (gate[rows, :] * combined).astype(BF16)
         out_copy(leaf).start()
 
-    @pl.when((z < PLANES - 1) & (y < 2))
+    @pl.when((z < PLANES - 1) & (y == 0))
+    def _():
+        pack_copy(48).wait_send()
+
+    @pl.when((z < PLANES - 1) & (y == 1))
     def _():
         pack_copy(64).wait_send()
 

time: 34.9 us -> 34.9 us (level)
  no operation moved by 1% of the time
where the time goes in v7:
time: 34.9 us; the launch traced here: 34.8 us
  Pallas kernels  32.9 us (94%)
  local copies, waits for them, and re-layouts  1.87 us (5%)
    pallas_call x1, Pallas kernels, per_device(): pl.pallas_call(body, out_shape=jax.ShapeDtypeStruct(tokens.shape, BF16),...  32.9 us
    unnamed x1, local copies, waits for them, and re-layouts  1.87 us

profile of v7, /device:TPU:224, one launch (start us, length us, event | category | flops | bytes accessed | tf_op | source)
XLA Modules:
  0.0 34.8 jit_solution(7447992286639915749)
XLA Ops:
  0.0 32.9 %shard_map.136 = bf16[1024,256]{1,0:T(8,128)(2,1)} custom-call(bf16[1024,256]{1,0:T(8,128)(2,1)} %tok.1, f32[1,1024]{1,0:T(1,128)} %bitcast.2, bf16[1024,256]{1,0:T(8,128)(2,1)} %w_value.1, bf16[1024,256]{1,0:T(8,128)(2,1)} %w_gate.1, f32[32,512]{1,0:T(8,128)} %phi.1, f32[32,256]{1,0:T(8,128)} %coeff.1, f32[1,256]{1,0:T(1,128)} %bitcast.3, f32[16,256]{1,0:T(8,128)} %up.1, ...), custom_call_target="tpu_custom_call" | custom-call | flops 4000000000 | bytes 8000000 | tf_op jit(solution)/shard_map/pallas_call | solution.py:730
  32.9 1.9 %copy.16 = bf16[1024,256]{1,0:T(8,128)(2,1)} copy(bf16[1024,256]{1,0:T(8,128)(2,1)} %shard_map.136) | data formatting | bytes 1048576

commit v8 on v7

--- a/solution.py
+++ b/solution.py
@@ -58,7 +58,7 @@
     g, w, gain_v, phi_v, coeff_v, skip_v, up_v, down_v, lift_v, spread_v, coup_v, fwd_f, inv_f, fwd_v, inv_v,
     vals, halo, gate, near, spec, khat, mom_m, lift_m, six_m, far_m, red_m, moms,
     m2, m2_prev, ctx_out, ctx_in, pack_out, pack_in, m5_in, far0, far1, out_v, parts, part_squares,
-    local_sem, gsend, drecv, rrecv, hsem, csem, s1, r1, s1p, r1p, s2, r2, s5, r5, ready_plane, ready_next, ready_edge, ready_later, osem,
+    local_sem, tsem, gsend, drecv, rrecv, hsem, csem, s1, r1, s1p, r1p, s2, r2, s5, r5, ready_plane, ready_next, ready_edge, ready_later, osem,
 ):
     t = lax.axis_index("tm")
     x = lax.axis_index("chan")
@@ -69,6 +69,13 @@
     rank = 2 * y + 1 - core
     right, left = lax.rem(x + 1, 4), lax.rem(x + 3, 4)
 
+    def own_tokens(group):
+        rows = pl.ds((1 - group) * 2 * LEAF, 2 * LEAF)
+        return pltpu.make_async_copy(tok.at[rows], g.at[0, rows], tsem.at[group])
+
+    for group in range(2):
+        own_tokens(group).start()
+
     barrier = pltpu.get_barrier_semaphore()
 
     def signal(semaphore, frames, chans):
@@ -106,7 +113,7 @@
     def direct(group, way):
         rows = pl.ds((1 - group) * 2 * LEAF, 2 * LEAF)
         return pltpu.make_async_remote_copy(
-            src_ref=tok.at[rows],
+            src_ref=g.at[0, rows],
             dst_ref=g.at[1 + way, rows],
             send_sem=gsend,
             recv_sem=drecv.at[way, group],
@@ -126,6 +133,7 @@
         )
 
     def send_direct(group):
+        own_tokens(group).wait()
         for way in range(2):
             direct(group, way).start()
 
@@ -292,7 +300,6 @@
         copies[name] = pltpu.make_async_copy(source, target, local_sem.at[len(copies)])
         copies[name].start()
 
-    local("tok", tok, g.at[0])
     for slot in range(4):
         rows = pl.ds(pl.multiple_of(owners[slot] * WIDTH, WIDTH), WIDTH)
         local(("v", slot), w_value.at[rows], w.at[slot, :, pl.ds(0, WIDTH)])
@@ -341,7 +348,7 @@
     for slot in range(4):
         copies["v", slot].wait()
         copies["g", slot].wait()
-    for name in ("tok", "gain", "skip", "coup", "inv"):
+    for name in ("gain", "skip", "coup", "inv"):
         copies[name].wait()
     pass_on(0)
     chain(4)
@@ -708,6 +715,7 @@
         vmem((frames, 2 * WIDTH), F32),
         vmem((frames, WIDTH // 2), F32),
         dma((20,)),
+        dma((2,)),
         dma(()),
         dma((2, 2)),
         dma((2, 2)),

time: 34.9 us -> 34.7 us (level)
  no operation moved by 1% of the time
where the time goes in v8:
time: 34.7 us; the launch traced here: 34.6 us
  Pallas kernels  32.7 us (94%)
  local copies, waits for them, and re-layouts  1.87 us (5%)
    pallas_call x1, Pallas kernels, per_device(): pl.pallas_call(body, out_shape=jax.ShapeDtypeStruct(tokens.shape, BF16),...  32.7 us
    unnamed x1, local copies, waits for them, and re-layouts  1.87 us

profile of v8, /device:TPU:224, one launch (start us, length us, event | category | flops | bytes accessed | tf_op | source)
XLA Modules:
  0.0 34.6 jit_solution(824732921339762776)
XLA Ops:
  0.0 32.7 %shard_map.136 = bf16[1024,256]{1,0:T(8,128)(2,1)} custom-call(bf16[1024,256]{1,0:T(8,128)(2,1)} %tok.1, f32[1,1024]{1,0:T(1,128)} %bitcast.2, bf16[1024,256]{1,0:T(8,128)(2,1)} %w_value.1, bf16[1024,256]{1,0:T(8,128)(2,1)} %w_gate.1, f32[32,512]{1,0:T(8,128)} %phi.1, f32[32,256]{1,0:T(8,128)} %coeff.1, f32[1,256]{1,0:T(1,128)} %bitcast.3, f32[16,256]{1,0:T(8,128)} %up.1, ...), custom_call_target="tpu_custom_call" | custom-call | flops 4000000000 | bytes 8000000 | tf_op jit(solution)/shard_map/pallas_call | solution.py:738
  32.7 1.9 %copy.16 = bf16[1024,256]{1,0:T(8,128)(2,1)} copy(bf16[1024,256]{1,0:T(8,128)(2,1)} %shard_map.136) | data formatting | bytes 1048576

commit v9 on v7

--- a/solution.py
+++ b/solution.py
@@ -461,6 +461,8 @@
         ctx_copy(1).start()
 
     gates_of(0)
+    spectra(0)
+    near_rows((1, 2))
 
     plane_all.wait_recv()
     stack = m2[...].reshape(PLANE * RANK, WIDTH)
@@ -508,14 +510,12 @@
     def _():
         pack_copy(32).start()
 
-    spectra(0)
-
     @pl.when(t > 0)
     def _():
         halo_copy.wait_recv()
 
     spec[LEAVES] = dot(fwd_v[...], jnp.concatenate([halo[...], halo[...]], 0))
-    near_rows((0, 1, 2))
+    near_rows((0,))
 
     @pl.when(t > 0)
     def _():

time: 34.9 us -> 34.9 us (level)
  no operation moved by 1% of the time
where the time goes in v9:
time: 34.9 us; the launch traced here: 34.8 us
  Pallas kernels  32.9 us (94%)
  local copies, waits for them, and re-layouts  1.87 us (5%)
    pallas_call x1, Pallas kernels, per_device(): pl.pallas_call(body, out_shape=jax.ShapeDtypeStruct(tokens.shape, BF16),...  32.9 us
    unnamed x1, local copies, waits for them, and re-layouts  1.87 us

profile of v9, /device:TPU:224, one launch (start us, length us, event | category | flops | bytes accessed | tf_op | source)
XLA Modules:
  0.0 34.8 jit_solution(3926299750949343719)
XLA Ops:
  0.0 32.9 %shard_map.136 = bf16[1024,256]{1,0:T(8,128)(2,1)} custom-call(bf16[1024,256]{1,0:T(8,128)(2,1)} %tok.1, f32[1,1024]{1,0:T(1,128)} %bitcast.2, bf16[1024,256]{1,0:T(8,128)(2,1)} %w_value.1, bf16[1024,256]{1,0:T(8,128)(2,1)} %w_gate.1, f32[32,512]{1,0:T(8,128)} %phi.1, f32[32,256]{1,0:T(8,128)} %coeff.1, f32[1,256]{1,0:T(1,128)} %bitcast.3, f32[16,256]{1,0:T(8,128)} %up.1, ...), custom_call_target="tpu_custom_call" | custom-call | flops 4000000000 | bytes 8000000 | tf_op jit(solution)/shard_map/pallas_call | solution.py:730
  32.9 1.9 %copy.16 = bf16[1024,256]{1,0:T(8,128)(2,1)} copy(bf16[1024,256]{1,0:T(8,128)(2,1)} %shard_map.136) | data formatting | bytes 1048576

commit v10 on v9

--- a/solution.py
+++ b/solution.py
@@ -567,6 +567,27 @@
     three = jnp.where(inside, m2[at], m2_prev[0]).astype(F32) * core.astype(F32)
     expansion = reduced(0, two, three)
 
+    for k in range(2, PLANES):
+
+        @pl.when(z >= k)
+        def _():
+            five_copy(k).wait_recv()
+
+    odd = lax.rem(z, 2)
+    expansion = expansion + reduced(
+        3, m5_in[2].astype(F32), m5_in[3].astype(F32) * odd.astype(F32)
+    )
+    pad = jnp.zeros((64, WIDTH), BF16)
+
+    def sixth(base):
+        pair = [m5_in[base], m5_in[base - 1]]
+        return dot(six_m[...], jnp.concatenate(pair + pair + [pad], 0))
+
+    odd_six = lax.rem(lax.div(z, 2), 2)
+    expansion = expansion + reduced(
+        4, sixth(4 + odd), sixth(6 + odd) * odd_six.astype(F32)
+    )
+
     @pl.when((z > 0) & (y == 0))
     def _():
         pack_copy(48).wait_recv()
@@ -590,27 +611,6 @@
     two = pack_in[pl.ds(pl.multiple_of(odd * RANK, RANK), RANK), :].astype(F32)
     three = pack_in[0:16, :].astype(F32) * odd.astype(F32)
     expansion = expansion + reduced(2, two, three)
-
-    for k in range(2, PLANES):
-
-        @pl.when(z >= k)
-        def _():
-            five_copy(k).wait_recv()
-
-    odd = lax.rem(z, 2)
-    expansion = expansion + reduced(
-        3, m5_in[2].astype(F32), m5_in[3].astype(F32) * odd.astype(F32)
-    )
-    pad = jnp.zeros((64, WIDTH), BF16)
-
-    def sixth(base):
-        pair = [m5_in[base], m5_in[base - 1]]
-        return dot(six_m[...], jnp.concatenate(pair + pair + [pad], 0))
-
-    odd_six = lax.rem(lax.div(z, 2), 2)
-    expansion = expansion + reduced(
-        4, sixth(4 + odd), sixth(6 + odd) * odd_six.astype(F32)
-    )
 
     expansion = expansion[:RANK] + expansion[RANK:]
 

time: 34.9 us -> 35 us (level)
  no operation moved by 1% of the time
where the time goes in v10:
time: 35 us; the launch traced here: 34.9 us
  Pallas kernels  33 us (94%)
  local copies, waits for them, and re-layouts  1.87 us (5%)
    pallas_call x1, Pallas kernels, per_device(): pl.pallas_call(body, out_shape=jax.ShapeDtypeStruct(tokens.shape, BF16),...  33 us
    unnamed x1, local copies, waits for them, and re-layouts  1.87 us

profile of v10, /device:TPU:224, one launch (start us, length us, event | category | flops | bytes accessed | tf_op | source)
XLA Modules:
  0.0 34.9 jit_solution(12192889348805799937)
XLA Ops:
  0.0 33.0 %shard_map.136 = bf16[1024,256]{1,0:T(8,128)(2,1)} custom-call(bf16[1024,256]{1,0:T(8,128)(2,1)} %tok.1, f32[1,1024]{1,0:T(1,128)} %bitcast.2, bf16[1024,256]{1,0:T(8,128)(2,1)} %w_value.1, bf16[1024,256]{1,0:T(8,128)(2,1)} %w_gate.1, f32[32,512]{1,0:T(8,128)} %phi.1, f32[32,256]{1,0:T(8,128)} %coeff.1, f32[1,256]{1,0:T(1,128)} %bitcast.3, f32[16,256]{1,0:T(8,128)} %up.1, ...), custom_call_target="tpu_custom_call" | custom-call | flops 4000000000 | bytes 8000000 | tf_op jit(solution)/shard_map/pallas_call | solution.py:730
  33.0 1.9 %copy.16 = bf16[1024,256]{1,0:T(8,128)(2,1)} copy(bf16[1024,256]{1,0:T(8,128)(2,1)} %shard_map.136) | data formatting | bytes 1048576

commit v11 on v9

--- a/solution.py
+++ b/solution.py
@@ -68,6 +68,9 @@
     own = lax.rem(t, PLANE)
     rank = 2 * y + 1 - core
     right, left = lax.rem(x + 1, 4), lax.rem(x + 3, 4)
+
+    def later(distance):
+        return lax.rem(t + distance, PLANES * PLANE)
 
     barrier = pltpu.get_barrier_semaphore()
 
@@ -376,7 +379,7 @@
         dst_ref=halo,
         send_sem=hsem.at[0],
         recv_sem=hsem.at[1],
-        device_id=(t + 1, x),
+        device_id=(later(1), x),
         device_id_type=MESH,
     )
 
@@ -387,7 +390,7 @@
             dst_ref=ctx_in.at[rows],
             send_sem=csem.at[0, part],
             recv_sem=csem.at[1, part],
-            device_id=(t + 1, x),
+            device_id=(later(1), x),
             device_id_type=MESH,
         )
 
@@ -445,7 +448,7 @@
             dst_ref=m2_prev.at[source],
             send_sem=s1p.at[target],
             recv_sem=r1p.at[source],
-            device_id=((z + 1) * PLANE + target, x),
+            device_id=(lax.rem(z + 1, PLANES) * PLANE + target, x),
             device_id_type=MESH,
         )
 
@@ -476,7 +479,7 @@
             dst_ref=pack_in.at[pl.ds(0, rows)],
             send_sem=s2,
             recv_sem=r2,
-            device_id=(t + PLANE, x),
+            device_id=(later(PLANE), x),
             device_id_type=MESH,
         )
 
@@ -486,7 +489,7 @@
             dst_ref=m5_in.at[k],
             send_sem=s5.at[k],
             recv_sem=r5.at[k],
-            device_id=(t + k * PLANE, x),
+            device_id=(later(k * PLANE), x),
             device_id_type=MESH,
         )
 
@@ -529,29 +532,6 @@
     far0[3] = gathered(0, moms[1, 0:16, :], moms[0, 0:16, :])
     far1[0] = gathered(1, prev[48:64])
     far1[1] = gathered(1, prev[32:48], prev[48:64])
-
-    gather_sent = g.at[pl.ds(0, 3)]
-    pltpu.make_async_remote_copy(
-        src_ref=gather_sent,
-        dst_ref=gather_sent,
-        send_sem=gsend,
-        recv_sem=drecv.at[0, 0],
-        device_id=(t, right),
-        device_id_type=MESH,
-    ).wait_send()
-
-    plane_all.wait_send()
-
-    @pl.when(t < PLANES * PLANE - 1)
-    def _():
-        halo_copy.wait_send()
-        ctx_copy(0).wait_send()
-        ctx_copy(1).wait_send()
-
-    @pl.when((y == 3) & (z < PLANES - 1))
-    def _():
-        for target in range(2):
-            next_plane_copy(target, core).wait_send()
 
     @pl.when((y == 0) & (z > 0))
     def _():
@@ -625,6 +605,29 @@
         combined = near[rows, :] + dot(far_m[leaf], whole)
         out_v[rows, :] = (gate[rows, :] * combined).astype(BF16)
         out_copy(leaf).start()
+
+    gather_sent = g.at[pl.ds(0, 3)]
+    pltpu.make_async_remote_copy(
+        src_ref=gather_sent,
+        dst_ref=gather_sent,
+        send_sem=gsend,
+        recv_sem=drecv.at[0, 0],
+        device_id=(t, right),
+        device_id_type=MESH,
+    ).wait_send()
+
+    plane_all.wait_send()
+
+    @pl.when(t < PLANES * PLANE - 1)
+    def _():
+        halo_copy.wait_send()
+        ctx_copy(0).wait_send()
+        ctx_copy(1).wait_send()
+
+    @pl.when((y == 3) & (z < PLANES - 1))
+    def _():
+        for target in range(2):
+            next_plane_copy(target, core).wait_send()
 
     @pl.when((z < PLANES - 1) & (y == 0))
     def _():

time: 34.9 us -> 34.9 us (level)
  no operation moved by 1% of the time
where the time goes in v11:
time: 34.9 us; the launch traced here: 34.8 us
  Pallas kernels  32.9 us (94%)
  local copies, waits for them, and re-layouts  1.87 us (5%)
    pallas_call x1, Pallas kernels, per_device(): pl.pallas_call(body, out_shape=jax.ShapeDtypeStruct(tokens.shape, BF16),...  32.9 us
    unnamed x1, local copies, waits for them, and re-layouts  1.87 us

profile of v11, /device:TPU:224, one launch (start us, length us, event | category | flops | bytes accessed | tf_op | source)
XLA Modules:
  0.0 34.8 jit_solution(7703174474162679324)
XLA Ops:
  0.0 32.9 %shard_map.136 = bf16[1024,256]{1,0:T(8,128)(2,1)} custom-call(bf16[1024,256]{1,0:T(8,128)(2,1)} %tok.1, f32[1,1024]{1,0:T(1,128)} %bitcast.2, bf16[1024,256]{1,0:T(8,128)(2,1)} %w_value.1, bf16[1024,256]{1,0:T(8,128)(2,1)} %w_gate.1, f32[32,512]{1,0:T(8,128)} %phi.1, f32[32,256]{1,0:T(8,128)} %coeff.1, f32[1,256]{1,0:T(1,128)} %bitcast.3, f32[16,256]{1,0:T(8,128)} %up.1, ...), custom_call_target="tpu_custom_call" | custom-call | flops 4000000000 | bytes 8000000 | tf_op jit(solution)/shard_map/pallas_call | solution.py:733
  32.9 1.9 %copy.16 = bf16[1024,256]{1,0:T(8,128)(2,1)} copy(bf16[1024,256]{1,0:T(8,128)(2,1)} %shard_map.136) | data formatting | bytes 1048576

commit v12 on v11

--- a/solution.py
+++ b/solution.py
@@ -411,8 +411,6 @@
         ctx_copy(0).start()
 
     spectra(2)
-    gates_of(2)
-    near_rows((3,))
 
     wait_relayed(1)
     values_of(0)
@@ -512,6 +510,9 @@
     @pl.when((z < PLANES - 1) & (y >= 2))
     def _():
         pack_copy(32).start()
+
+    gates_of(2)
+    near_rows((3,))
 
     @pl.when(t > 0)
     def _():

time: 34.9 us -> 34.9 us (level)
  no operation moved by 1% of the time
where the time goes in v12:
time: 34.9 us; the launch traced here: 34.8 us
  Pallas kernels  32.9 us (94%)
  local copies, waits for them, and re-layouts  1.87 us (5%)
    pallas_call x1, Pallas kernels, per_device(): pl.pallas_call(body, out_shape=jax.ShapeDtypeStruct(tokens.shape, BF16),...  32.9 us
    unnamed x1, local copies, waits for them, and re-layouts  1.87 us

profile of v12, /device:TPU:224, one launch (start us, length us, event | category | flops | bytes accessed | tf_op | source)
XLA Modules:
  0.0 34.8 jit_solution(12658528565773272309)
XLA Ops:
  0.0 32.9 %shard_map.136 = bf16[1024,256]{1,0:T(8,128)(2,1)} custom-call(bf16[1024,256]{1,0:T(8,128)(2,1)} %tok.1, f32[1,1024]{1,0:T(1,128)} %bitcast.2, bf16[1024,256]{1,0:T(8,128)(2,1)} %w_value.1, bf16[1024,256]{1,0:T(8,128)(2,1)} %w_gate.1, f32[32,512]{1,0:T(8,128)} %phi.1, f32[32,256]{1,0:T(8,128)} %coeff.1, f32[1,256]{1,0:T(1,128)} %bitcast.3, f32[16,256]{1,0:T(8,128)} %up.1, ...), custom_call_target="tpu_custom_call" | custom-call | flops 4000000000 | bytes 8000000 | tf_op jit(solution)/shard_map/pallas_call | solution.py:734
  32.9 1.9 %copy.16 = bf16[1024,256]{1,0:T(8,128)(2,1)} copy(bf16[1024,256]{1,0:T(8,128)(2,1)} %shard_map.136) | data formatting | bytes 1048576

commit v13 on v11

--- a/solution.py
+++ b/solution.py
@@ -334,8 +334,8 @@
                 signal(ready_later, t - PLANE, x)
 
     chain(0)
+    send_direct(1)
     tables_near()
-    send_direct(1)
     chain(1)
     tables_moments()
     chain(2)

time: 34.9 us -> 34.9 us (level)
  no operation moved by 1% of the time
where the time goes in v13:
time: 34.9 us; the launch traced here: 34.8 us
  Pallas kernels  32.9 us (94%)
  local copies, waits for them, and re-layouts  1.87 us (5%)
    pallas_call x1, Pallas kernels, per_device(): pl.pallas_call(body, out_shape=jax.ShapeDtypeStruct(tokens.shape, BF16),...  32.9 us
    unnamed x1, local copies, waits for them, and re-layouts  1.87 us

profile of v13, /device:TPU:224, one launch (start us, length us, event | category | flops | bytes accessed | tf_op | source)
XLA Modules:
  0.0 34.8 jit_solution(11451416515454361923)
XLA Ops:
  0.0 32.9 %shard_map.136 = bf16[1024,256]{1,0:T(8,128)(2,1)} custom-call(bf16[1024,256]{1,0:T(8,128)(2,1)} %tok.1, f32[1,1024]{1,0:T(1,128)} %bitcast.2, bf16[1024,256]{1,0:T(8,128)(2,1)} %w_value.1, bf16[1024,256]{1,0:T(8,128)(2,1)} %w_gate.1, f32[32,512]{1,0:T(8,128)} %phi.1, f32[32,256]{1,0:T(8,128)} %coeff.1, f32[1,256]{1,0:T(1,128)} %bitcast.3, f32[16,256]{1,0:T(8,128)} %up.1, ...), custom_call_target="tpu_custom_call" | custom-call | flops 4000000000 | bytes 8000000 | tf_op jit(solution)/shard_map/pallas_call | solution.py:733
  32.9 1.9 %copy.16 = bf16[1024,256]{1,0:T(8,128)(2,1)} copy(bf16[1024,256]{1,0:T(8,128)(2,1)} %shard_map.136) | data formatting | bytes 1048576
